TPU v7x, 32 devices: a whole 2x2x4 slice. The times are simulated.
32 devices in a mesh: fsdp: 16 (over z, x, core), tp: 2 (over y).
Axes of the slice: x: 2, y: 2, z: 4, core: 2. Of those that a mesh axis runs over, the one named last changes fastest.
Arguments:
- hidden_in: bfloat16 [32, 512, 1024], P('fsdp', 'tp'), may hold values from -6 to 6
- segment_ids: int32 [32, 512], P('fsdp'), may hold values from 0 to 3, never falling along the last dimension, each value on 1 to 256 neighbouring positions
- norm_gain: bfloat16 [2, 1024], P(None, 'fsdp'), may hold values from 0.5 to 1.5
- norm_bias: bfloat16 [2, 1024], P(None, 'fsdp'), may hold values from -1.75 to 1.75
- qkv_weight: bfloat16 [1024, 3, 1024], P('fsdp', None, 'tp'), may hold values from -0.1875 to 0.1875
- qkv_bias: bfloat16 [3, 1024], P(None, ('tp', 'fsdp')), may hold values from -1.75 to 1.75
- dense_weight: bfloat16 [1024, 1024], P('fsdp', 'tp'), may hold values from -0.75 to 0.75
- mlp_in_weight: bfloat16 [1024, 4096], P('fsdp', 'tp'), may hold values from -0.1875 to 0.1875
- mlp_in_bias: bfloat16 [4096], P(('tp', 'fsdp')), may hold values from -1.75 to 1.75
- mlp_out_weight: bfloat16 [1024, 4096], P('fsdp', 'tp'), may hold values from -0.1875 to 0.1875
- out_bias: bfloat16 [2, 1024], P(None, 'fsdp'), may hold values from -1.75 to 1.75
- out_grad: bfloat16 [32, 512, 1024], P('fsdp', 'tp'), may hold values from -6 to 6
Outputs:
- hidden_out: bfloat16 [32, 512, 1024], P('fsdp', 'tp')
- input_grad: float32 [32, 512, 1024], P('fsdp', 'tp')
- norm_gain_grad: float32 [2, 1024], P(None, 'fsdp')
- norm_bias_grad: float32 [2, 1024], P(None, 'fsdp')
- qkv_weight_grad: float32 [1024, 3, 1024], P('fsdp', None, 'tp')
- qkv_bias_grad: float32 [3, 1024], P(None, ('tp', 'fsdp'))
- dense_weight_grad: float32 [1024, 1024], P('fsdp', 'tp')
- mlp_in_weight_grad: float32 [1024, 4096], P('fsdp', 'tp')
- mlp_in_bias_grad: float32 [4096], P(('tp', 'fsdp'))
- mlp_out_weight_grad: float32 [1024, 4096], P('fsdp', 'tp')
- out_bias_grad: float32 [2, 1024], P(None, 'fsdp')
Inputs may be any that keep to these rules, and one draw needn't show every extreme that they name: `segment_ids`: within each row of 512 tokens the ids never fall, every id of 0 to 3 occurs as one run, and the longest run has exactly 256 tokens.
All inputs are finite; a program needn't handle non-finite values.
Results may differ from a plain program's by a relative error of at most 0.03.
Values may be sent and summed in bfloat16 or wider, within the bound.
A program may use at most 128 MiB of HBM per device.

v0:
```python
import math

import jax
import jax.numpy as jnp
from jax import lax
from jax.sharding import PartitionSpec as P

HEAD_DIM = 64
ROT_DIM = 16


norm_eps = 1e-05
masked_fill = -1e30


def layer_norm(row_values, gain_row, shift_row):
    average = jnp.mean(row_values, axis=-1, keepdims=True)
    centered = row_values - average
    variance = jnp.mean(centered * centered, axis=-1, keepdims=True)
    return centered * lax.rsqrt(variance + norm_eps) * gain_row + shift_row


def rotary_tables(segment_rows):
    row_width = segment_rows.shape[-1]
    places = jnp.arange(row_width, dtype=jnp.int32)
    same_doc = segment_rows[..., :, None] == segment_rows[..., None, :]
    allowed = jnp.logical_and(same_doc, places[None, :] <= places[:, None])
    positions = jnp.sum(allowed.astype(jnp.int32), axis=-1) - 1
    half_dim = ROT_DIM // 2
    frequency = jnp.exp(
        jnp.arange(half_dim, dtype=jnp.float32) * (-2.0 * math.log(10000.0) / ROT_DIM)
    )
    angles = positions.astype(jnp.float32)[..., None] * frequency
    cosine_table = jnp.concatenate([jnp.cos(angles), jnp.cos(angles)], axis=-1)[..., None, :]
    sine_table = jnp.concatenate([jnp.sin(angles), jnp.sin(angles)], axis=-1)[..., None, :]
    return (cosine_table, sine_table, allowed)


def rotate(vectors, cosine_table, sine_table):
    half_dim = ROT_DIM // 2
    first_half = vectors[..., :half_dim]
    second_half = vectors[..., half_dim:ROT_DIM]
    flipped = jnp.concatenate([-second_half, first_half], axis=-1)
    turned = vectors[..., :ROT_DIM] * cosine_table + flipped * sine_table
    return jnp.concatenate([turned, vectors[..., ROT_DIM:]], axis=-1)


def gelu_exact(pre_act):
    return jax.nn.gelu(pre_act, approximate=False)


def attend(pieces):
    queries, key_rows, value_rows, allowed = pieces
    scale = HEAD_DIM ** (-0.5)
    scores = (
        jnp.einsum("qhe,khe->hqk", queries, key_rows, preferred_element_type=jnp.float32) * scale
    )
    masked = jnp.where(allowed[None], scores, masked_fill)
    largest = jnp.max(masked, axis=-1, keepdims=True)
    expanded = jnp.exp(masked - largest)
    summed = jnp.sum(expanded, axis=-1, keepdims=True)
    weights = (expanded / summed).astype(jnp.bfloat16)
    mixed_rows = jnp.einsum("hqk,khe->qhe", weights, value_rows, preferred_element_type=jnp.float32)
    return (mixed_rows.astype(jnp.bfloat16), largest + jnp.log(summed))


def attend_back(pieces):
    queries, key_rows, value_rows, allowed, log_total, mixed_grad = pieces
    scale = HEAD_DIM ** (-0.5)
    scores = (
        jnp.einsum("qhe,khe->hqk", queries, key_rows, preferred_element_type=jnp.float32) * scale
    )
    masked = jnp.where(allowed[None], scores, masked_fill)
    weights = jnp.exp(masked - log_total)
    weight_grad = jnp.einsum(
        "qhe,khe->hqk", mixed_grad, value_rows, preferred_element_type=jnp.float32
    )
    value_grad = jnp.einsum(
        "hqk,qhe->khe", weights.astype(jnp.bfloat16), mixed_grad, preferred_element_type=jnp.float32
    )
    inner = jnp.sum(weights * weight_grad, axis=-1, keepdims=True)
    score_grad = (weights * (weight_grad - inner)).astype(jnp.bfloat16)
    query_grad = (
        jnp.einsum("hqk,khe->qhe", score_grad, key_rows, preferred_element_type=jnp.float32) * scale
    )
    key_grad = (
        jnp.einsum("hqk,qhe->khe", score_grad, queries, preferred_element_type=jnp.float32) * scale
    )
    return (query_grad, key_grad, value_grad)


def on_device(
    hidden_in,
    segment_ids,
    norm_gain,
    norm_bias,
    qkv_weight,
    qkv_bias,
    dense_weight,
    mlp_in_weight,
    mlp_in_bias,
    mlp_out_weight,
    out_bias,
    out_grad,
):
    gathered = (
        lax.all_gather(qkv_weight, "fsdp", axis=0, tiled=True),
        lax.all_gather(qkv_bias, "fsdp", axis=1, tiled=True),
        lax.all_gather(dense_weight, "fsdp", axis=0, tiled=True),
        lax.all_gather(mlp_in_weight, "fsdp", axis=0, tiled=True),
        lax.all_gather(mlp_in_bias, "fsdp", axis=0, tiled=True),
        lax.all_gather(mlp_out_weight, "fsdp", axis=0, tiled=True),
        lax.all_gather(norm_gain, "fsdp", axis=1, tiled=True),
        lax.all_gather(norm_bias, "fsdp", axis=1, tiled=True),
        lax.all_gather(out_bias, "fsdp", axis=1, tiled=True),
    )
    (
        qkv_full,
        qkv_shift,
        dense_full,
        in_full,
        in_shift,
        out_full,
        gain_full,
        bias_full,
        out_shift,
    ) = gathered
    gains = gain_full.astype(jnp.float32)
    shifts = bias_full.astype(jnp.float32)
    seq_count, local_len, model_width = hidden_in.shape
    row_len = segment_ids.shape[1]
    token_count = seq_count * row_len
    local_rows = hidden_in.astype(jnp.float32)
    attn_local = layer_norm(local_rows, gains[0], shifts[0]).astype(jnp.bfloat16)
    mlp_local = layer_norm(local_rows, gains[1], shifts[1]).astype(jnp.bfloat16)
    attn_in, mlp_input = (
        lax.all_gather(attn_local, "tp", axis=1, tiled=True),
        lax.all_gather(mlp_local, "tp", axis=1, tiled=True),
    )
    attn_flat = attn_in.reshape(token_count, model_width)
    mlp_flat = mlp_input.reshape(token_count, model_width)
    cosine_table, sine_table, allowed = rotary_tables(segment_ids)
    projected = jnp.einsum(
        "nd,dje->nje", attn_flat, qkv_full, preferred_element_type=jnp.float32
    ) + qkv_shift.astype(jnp.float32)
    local_width = projected.shape[-1]
    head_shape = (seq_count, row_len, local_width // HEAD_DIM, HEAD_DIM)
    query_turned, turn_pull = jax.vjp(
        lambda vectors: rotate(vectors, cosine_table, sine_table),
        projected[:, 0].reshape(head_shape),
    )
    queries = query_turned.astype(jnp.bfloat16)
    key_rows = rotate(projected[:, 1].reshape(head_shape), cosine_table, sine_table).astype(
        jnp.bfloat16
    )
    value_rows = projected[:, 2].reshape(head_shape).astype(jnp.bfloat16)
    mixed_heads, log_total = lax.map(attend, (queries, key_rows, value_rows, allowed))
    mixed_flat = mixed_heads.reshape(token_count, local_width)
    attn_part = jnp.einsum("ne,de->nd", mixed_flat, dense_full, preferred_element_type=jnp.float32)
    pre_act = jnp.dot(mlp_flat, in_full, preferred_element_type=jnp.float32) + in_shift.astype(
        jnp.float32
    )
    activated, gelu_pull = jax.vjp(gelu_exact, pre_act)
    act_low = activated.astype(jnp.bfloat16)
    mlp_part = jnp.einsum("nf,df->nd", act_low, out_full, preferred_element_type=jnp.float32)
    partial_sum = (attn_part + mlp_part).reshape(seq_count, row_len, model_width)
    branches = lax.psum_scatter(
        partial_sum.astype(jnp.bfloat16), "tp", scatter_dimension=1, tiled=True
    ).astype(jnp.float32)
    out_shift_wide = out_shift.astype(jnp.float32)
    hidden_out = (local_rows + branches + out_shift_wide[0] + out_shift_wide[1]).astype(
        jnp.bfloat16
    )
    grad_local = out_grad.astype(jnp.float32)
    grad_flat = lax.all_gather(out_grad, "tp", axis=1, tiled=True).reshape(token_count, model_width)
    act_grad = jnp.dot(grad_flat, out_full, preferred_element_type=jnp.float32)
    pre_grad = gelu_pull(act_grad)[0].astype(jnp.bfloat16)
    out_weight_grad = jnp.einsum(
        "nd,nf->df", grad_flat, act_low, preferred_element_type=jnp.float32
    )
    in_weight_grad = jnp.einsum("nd,nf->df", mlp_flat, pre_grad, preferred_element_type=jnp.float32)
    in_bias_grad = jnp.sum(pre_grad.astype(jnp.float32), axis=0)
    mlp_input_grad = jnp.einsum("nf,df->nd", pre_grad, in_full, preferred_element_type=jnp.float32)
    mixed_grad = jnp.einsum(
        "nd,de->ne", grad_flat, dense_full, preferred_element_type=jnp.float32
    ).astype(jnp.bfloat16)
    dense_grad = jnp.einsum("nd,ne->de", grad_flat, mixed_flat, preferred_element_type=jnp.float32)
    query_grad, key_grad, value_grad = lax.map(
        attend_back,
        (queries, key_rows, value_rows, allowed, log_total, mixed_grad.reshape(head_shape)),
    )
    projected_grad = jnp.stack(
        [
            turn_pull(query_grad)[0].reshape(token_count, local_width),
            turn_pull(key_grad)[0].reshape(token_count, local_width),
            value_grad.reshape(token_count, local_width),
        ],
        axis=1,
    ).astype(jnp.bfloat16)
    qkv_grad = jnp.einsum(
        "nd,nje->dje", attn_flat, projected_grad, preferred_element_type=jnp.float32
    )
    qkv_bias_grad = jnp.sum(projected_grad.astype(jnp.float32), axis=0)
    attn_input_grad = jnp.einsum(
        "nje,dje->nd", projected_grad, qkv_full, preferred_element_type=jnp.float32
    )
    bias_sum = jnp.sum(grad_local, axis=(0, 1))
    attn_back, mlp_back = (
        lax.psum_scatter(
            attn_input_grad.reshape(seq_count, row_len, model_width).astype(jnp.bfloat16),
            "tp",
            scatter_dimension=1,
            tiled=True,
        ).astype(jnp.float32),
        lax.psum_scatter(
            mlp_input_grad.reshape(seq_count, row_len, model_width).astype(jnp.bfloat16),
            "tp",
            scatter_dimension=1,
            tiled=True,
        ).astype(jnp.float32),
    )
    first_rows, first_gain, first_shift = jax.vjp(layer_norm, local_rows, gains[0], shifts[0])[1](
        attn_back
    )
    second_rows, second_gain, second_shift = jax.vjp(layer_norm, local_rows, gains[1], shifts[1])[
        1
    ](mlp_back)
    input_grad = grad_local + first_rows + second_rows
    vector_grads = jnp.stack([first_gain, second_gain, first_shift, second_shift, bias_sum])
    vector_total = lax.psum(vector_grads, "tp")
    (
        qkv_grad,
        qkv_bias_grad,
        dense_grad,
        in_weight_grad,
        in_bias_grad,
        out_weight_grad,
        vector_total,
    ) = (
        lax.psum_scatter(
            qkv_grad.astype(jnp.bfloat16), "fsdp", scatter_dimension=0, tiled=True
        ).astype(jnp.float32),
        lax.psum_scatter(
            qkv_bias_grad.astype(jnp.bfloat16), "fsdp", scatter_dimension=1, tiled=True
        ).astype(jnp.float32),
        lax.psum_scatter(
            dense_grad.astype(jnp.bfloat16), "fsdp", scatter_dimension=0, tiled=True
        ).astype(jnp.float32),
        lax.psum_scatter(
            in_weight_grad.astype(jnp.bfloat16), "fsdp", scatter_dimension=0, tiled=True
        ).astype(jnp.float32),
        lax.psum_scatter(
            in_bias_grad.astype(jnp.bfloat16), "fsdp", scatter_dimension=0, tiled=True
        ).astype(jnp.float32),
        lax.psum_scatter(
            out_weight_grad.astype(jnp.bfloat16), "fsdp", scatter_dimension=0, tiled=True
        ).astype(jnp.float32),
        lax.psum_scatter(
            vector_total.astype(jnp.bfloat16), "fsdp", scatter_dimension=1, tiled=True
        ).astype(jnp.float32),
    )
    out_bias_grad = jnp.stack([vector_total[4], vector_total[4]])
    return (
        hidden_out,
        input_grad,
        vector_total[0:2],
        vector_total[2:4],
        qkv_grad,
        qkv_bias_grad,
        dense_grad,
        in_weight_grad,
        in_bias_grad,
        out_weight_grad,
        out_bias_grad,
    )


def solution(mesh):
    in_specs = (
        P("fsdp", "tp", None),
        P("fsdp", None),
        P(None, "fsdp"),
        P(None, "fsdp"),
        P("fsdp", None, "tp"),
        P(None, ("tp", "fsdp")),
        P("fsdp", "tp"),
        P("fsdp", "tp"),
        P(("tp", "fsdp")),
        P("fsdp", "tp"),
        P(None, "fsdp"),
        P("fsdp", "tp", None),
    )
    out_specs = (
        P("fsdp", "tp", None),
        P("fsdp", "tp", None),
        P(None, "fsdp"),
        P(None, "fsdp"),
        P("fsdp", None, "tp"),
        P(None, ("tp", "fsdp")),
        P("fsdp", "tp"),
        P("fsdp", "tp"),
        P(("tp", "fsdp")),
        P("fsdp", "tp"),
        P(None, "fsdp"),
    )
    return jax.shard_map(
        on_device, mesh=mesh, in_specs=in_specs, out_specs=out_specs, check_vma=False
    )
```

profile of v0, /device:TPU:0, one launch (start us, length us, event | category | flops | bytes accessed | tf_op | source)
XLA Modules:
  0.0 885.4 jit_solution(18151446844319417089)
XLA Ops:
  8.7 23.1 %all-gather = bf16[16,64,2]{1,2,0:T(2,128)(2,1)S(1)} all-gather(bf16[1,64,2]{1,2,0:T(2,128)(2,1)} %bitcast.237), channel_id=1, replica_groups=mesh['fsdp'=16,'tp'=2] {'fsdp'}, dimensions={0}, use_global_device_ids=true | all-gather | bytes 4352 | tf_op jit(solution)/shard_map/all_gather | solution.py:113
  31.9 17.5 %all-gather.1 = bf16[16,64,2]{1,2,0:T(2,128)(2,1)S(1)} all-gather(bf16[1,64,2]{1,2,0:T(2,128)(2,1)} %bitcast.238), channel_id=1, replica_groups=mesh['fsdp'=16,'tp'=2] {'fsdp'}, dimensions={0}, use_global_device_ids=true | all-gather | bytes 4352 | tf_op jit(solution)/shard_map/all_gather | solution.py:114
  53.3 3.2 fusion.70
  60.0 18.8 %all-gather.2 = bf16[16,32,3]{1,2,0:T(4,128)(2,1)S(1)} all-gather(bf16[1,32,3]{1,2,0:T(4,128)(2,1)S(1)} %bitcast.236), channel_id=1, replica_groups=mesh['fsdp'=16,'tp'=2] {'fsdp'}, dimensions={0}, use_global_device_ids=true | all-gather | bytes 3264 | tf_op jit(solution)/shard_map/all_gather | solution.py:108
  78.9 17.3 %all-gather.3 = bf16[16,1,128]{2,1,0:T(2,128)(2,1)S(1)} all-gather(bf16[1,1,128]{2,1,0:T(2,128)(2,1)S(1)} %bitcast.239), channel_id=1, replica_groups=mesh['fsdp'=16,'tp'=2] {'fsdp'}, dimensions={0}, use_global_device_ids=true | all-gather | bytes 4352 | tf_op jit(solution)/shard_map/all_gather | solution.py:111
  97.5 4.1 convolution_convert_fusion.4
  106.7 13.1 %all-gather.13.cloned.1.call-done = bf16[2,512,1024]{2,1,0:T(8,128)(2,1)} async-done(((bf16[2,256,1024]{2,1,0:T(8,128)(2,1)}), bf16[2,512,1024]{2,1,0:T(8,128)(2,1)}) %all-gather.13.cloned.1.call-update) | async-done | bytes 2097168 | tf_op jit(solution)/shard_map/all_gather | solution.py:137
  119.7 47.5 %all-gather.15.cloned.1.call-done = bf16[1024,3,512]{2,0,1:T(8,128)(2,1)} async-done(((bf16[64,3,512]{2,0,1:T(8,128)(2,1)}), bf16[1024,3,512]{2,0,1:T(8,128)(2,1)}) %all-gather.15.cloned.1.call-update) | async-done | bytes 3145744 | tf_op jit(solution)/shard_map/all_gather | solution.py:107
  167.3 5.9 broadcast_add_fusion
  184.1 3.0 reshape_squeeze.8
  199.2 3.9 reshape.185
  203.1 3.3 copy.116
  206.4 13.1 %while.26 = (s32[]{:T(128)}, bf16[2,512,8,64]{1,3,2,0:T(8,128)(2,1)}, f32[2,8,512,1]{2,1,3,0:T(8,128)S(1)}, bf16[2,512,8,64]{1,3,2,0:T(8,128)(2,1)}, pred[2,512,...) while((s32[]{:T(128)}, ...), condition=%wide.region_6.7_spmd, body=%wide.region_3.6_spmd.sunk | while | flops 562294784 | bytes 32901240 | solution.py:157
  209.7 3.2 fusion.142
  216.2 3.2 fusion.142
  219.4 123.8 %while.27 = (s32[]{:T(128)}, f32[2,512,8,64]{1,0,3,2:T(2,128)}, f32[2,512,8,64]{1,0,3,2:T(2,128)}, bf16[2,512,8,64]{1,3,2,0:T(8,128)(2,1)}, bf16[2,512,8,64]{1,3...) while((s32[]{:T(128)}, f32[2,512,8,64]{1,0,3,2:T(2,128)}, ...), condition=%wide.region_10.11_spmd, body=%wide.region_8.10_spmd.sunk | while | flops 1374154752 | bytes 142462256 | solution.py:188
  221.4 2.9 multiply_reduce_fusion.2
  231.4 19.5 %dynamic_update_slice.30 = f32[2,512,8,64]{1,0,3,2:T(2,128)} dynamic-update-slice(f32[2,512,8,64]{1,0,3,2:T(2,128)} %get-tuple-element.460, f32[1,512,8,64]{1,0,3,2:T(1,128)S(1)} %copy.188, s32[]{:T(128)} %get-tuple-element.458, s32[]{:T(128)} %constant.64.clone.1..sunk, s32[]{:T(128)} %constant.64.clone.1..sunk, s32[]{:T(128)} %constant.64.clone.1..sunk) | dynamic-update-slice | bytes 2097156 | tf_op jit(solution)/shard_map/while/body/jit(dynamic_update_index_in_dim)/dynamic_update_slice | solution.py:188
  250.9 3.1 fusion.152
  255.1 19.6 %dynamic_update_slice.29 = f32[2,512,8,64]{1,0,3,2:T(2,128)} dynamic-update-slice(f32[2,512,8,64]{1,0,3,2:T(2,128)} %get-tuple-element.459, f32[1,512,8,64]{1,0,3,2:T(1,128)S(1)} %copy.187, s32[]{:T(128)} %get-tuple-element.458, s32[]{:T(128)} %constant.64.clone.1..sunk, s32[]{:T(128)} %constant.64.clone.1..sunk, s32[]{:T(128)} %constant.64.clone.1..sunk) | dynamic-update-slice | bytes 2097156 | tf_op jit(solution)/shard_map/while/body/jit(dynamic_update_index_in_dim)/dynamic_update_slice | solution.py:188
  274.7 6.6 fusion.154
  293.1 19.6 %dynamic_update_slice.30 = f32[2,512,8,64]{1,0,3,2:T(2,128)} dynamic-update-slice(f32[2,512,8,64]{1,0,3,2:T(2,128)} %get-tuple-element.460, f32[1,512,8,64]{1,0,3,2:T(1,128)S(1)} %copy.188, s32[]{:T(128)} %get-tuple-element.458, s32[]{:T(128)} %constant.64.clone.1..sunk, s32[]{:T(128)} %constant.64.clone.1..sunk, s32[]{:T(128)} %constant.64.clone.1..sunk) | dynamic-update-slice | bytes 2097156 | tf_op jit(solution)/shard_map/while/body/jit(dynamic_update_index_in_dim)/dynamic_update_slice | solution.py:188
  312.6 3.0 fusion.152
  316.7 19.6 %dynamic_update_slice.29 = f32[2,512,8,64]{1,0,3,2:T(2,128)} dynamic-update-slice(f32[2,512,8,64]{1,0,3,2:T(2,128)} %get-tuple-element.459, f32[1,512,8,64]{1,0,3,2:T(1,128)S(1)} %copy.187, s32[]{:T(128)} %get-tuple-element.458, s32[]{:T(128)} %constant.64.clone.1..sunk, s32[]{:T(128)} %constant.64.clone.1..sunk, s32[]{:T(128)} %constant.64.clone.1..sunk) | dynamic-update-slice | bytes 2097156 | tf_op jit(solution)/shard_map/while/body/jit(dynamic_update_index_in_dim)/dynamic_update_slice | solution.py:188
  336.3 6.6 fusion.154
  361.8 7.4 bitcast_convert_fusion
  369.3 10.6 %fusion.97 = f32[1024,2048]{1,0:T(8,128)} fusion(bf16[1024,1024]{1,0:T(8,128)(2,1)} %bitcast.245, bf16[1024,2048]{1,0:T(8,128)(2,1)} %all-gather.21.cloned.1.call-done), kind=kOutput, calls=%fused_computation.178 | convolution fusion | flops 4294967296 | bytes 14680064 | tf_op jit(solution)/shard_map/dot_general | solution.py:160
  379.9 27.8 %fusion.90 = (bf16[2048]{0:T(1024)(128)(2,1)S(1)}, bf16[1024,2048]{1,0:T(8,128)(2,1)S(1)}, f32[1024,2048]{1,0:T(8,128)}) fusion(f32[1024,2048]{1,0:T(8,128)} %fusion.97, f32[2048]{0:T(1024)S(1)} %bitcast.219, bf16[1024,1024]{1,0:T(8,128)(2,1)} %bitcast.242, bf16[1024,2048]{1,0:T(8,128)(2,1)} %all-gather.23.cloned.1.call-done), kind=kOutput, calls=%fused_computation.172 | convolution fusion | flops 4450154496 | bytes 27275264 | tf_op jit(solution)/shard_map/dot_general | solution.py:176
  407.8 5.7 convolution_convert_fusion.2
  417.1 8.7 multiply_convert_fusion.1
  425.8 8.2 fusion.98
  438.4 3.2 fusion.81
  443.1 7.1 convolution_convert_fusion.1
  450.3 18.8 %all-gather.4 = bf16[16,64,2]{1,2,0:T(2,128)(2,1)S(1)} all-gather(bf16[1,64,2]{1,2,0:T(2,128)(2,1)S(1)} %bitcast.240), channel_id=1, replica_groups=mesh['fsdp'=16,'tp'=2] {'fsdp'}, dimensions={0}, use_global_device_ids=true | all-gather | bytes 4352 | tf_op jit(solution)/shard_map/all_gather | solution.py:115
  472.1 3.5 fusion.80
  475.7 3.0 reduce-scatter.18.cloned.1.call-done
  478.7 4.4 convert_reduce_fusion.3
  483.1 7.2 psum.7
  491.2 9.5 %convert_bitcast_fusion = bf16[1024,2048]{0,1:T(8,128)(2,1)} fusion(bf16[1024,2048]{1,0:T(8,128)(2,1)} %copy-done.12, bf16[1024,1024]{1,0:T(8,128)(2,1)} %bitcast.244), kind=kOutput, calls=%fused_computation.77 | convolution fusion | flops 4297064448 | bytes 10485760 | tf_op jit(solution)/shard_map/nd,nf->df/dot_general | solution.py:178
  500.7 6.5 copy.152
  508.9 8.4 convolution_convert_fusion
  519.1 19.1 %reduce-scatter.30.cloned.1.call-done = bf16[32,3]{1,0:T(8,128)(2,1)} async-done(((bf16[512,3]{1,0:T(8,128)(2,1)}), bf16[32,3]{1,0:T(8,128)(2,1)}) %reduce-scatter.30.cloned.1.call-update) | async-done | bytes 208
  539.6 59.0 %reduce-scatter.32.cloned.1.call-done = bf16[64,512]{1,0:T(8,128)(2,1)} async-done(((bf16[1024,512]{1,0:T(8,128)(2,1)}), bf16[64,512]{1,0:T(8,128)(2,1)}) %reduce-scatter.32.cloned.1.call-update) | async-done | bytes 65552
  600.4 29.5 %all-reduce.8 = bf16[2048]{0:T(1024)(128)(2,1)S(1)} all-reduce(bf16[2048]{0:T(1024)(128)(2,1)S(1)} %get-tuple-element.264), channel_id=10, replica_groups=mesh['fsdp'=16,'tp'=2] {'fsdp'}, use_global_device_ids=true, to_apply=%region_30.31.clone | all-reduce | flops 2048 | bytes 8192
  630.5 37.1 %reduce-scatter.24.cloned.1.call-done = bf16[64,3,512]{2,0,1:T(8,128)(2,1)} async-done(((bf16[1024,3,512]{2,0,1:T(8,128)(2,1)}), bf16[64,3,512]{2,0,1:T(8,128)(2,1)}) %reduce-scatter.24.cloned.1.call-update) | async-done | bytes 196624 | tf_op jit(solution)/shard_map/reduce_scatter | solution.py:240
  669.2 56.5 %reduce-scatter.28.cloned.1.call-done = bf16[64,5]{1,0:T(8,128)(2,1)} async-done(((bf16[1024,5]{1,0:T(8,128)(2,1)}), bf16[64,5]{1,0:T(8,128)(2,1)}) %reduce-scatter.28.cloned.1.call-update) | async-done | bytes 656
  727.7 73.2 %reduce-scatter.34.cloned.1.call-done = bf16[64,2048]{1,0:T(8,128)(2,1)} async-done(((bf16[1024,2048]{1,0:T(8,128)(2,1)}), bf16[64,2048]{1,0:T(8,128)(2,1)}) %reduce-scatter.34.cloned.1.call-update) | async-done | bytes 262160
  803.1 73.6 %reduce-scatter.26.cloned.1.call-done = bf16[64,2048]{1,0:T(8,128)(2,1)} async-done(((bf16[1024,2048]{1,0:T(8,128)(2,1)}), bf16[64,2048]{1,0:T(8,128)(2,1)}) %reduce-scatter.26.cloned.1.call-update) | async-done | bytes 262160 | tf_op jit(solution)/shard_map/reduce_scatter | solution.py:249
  (241 shorter events, 113.0 us)
Async XLA Ops:
  7.2 90.3 %all-gather.17.cloned.1.call-start = ((), (), s32[]{:S(2)}) async-start(), calls=%async_computation.11 | async-start | bytes 1114112 | tf_op jit(solution)/shard_map/all_gather | solution.py:109
  7.9 89.6 %all-gather.25.cloned.1.call-start = ((), (), s32[]{:S(2)}) async-start(), calls=%async_computation.16 | async-start | bytes 3145728 | tf_op jit(solution)/shard_map/all_gather | solution.py:175
  8.7 111.1 %all-gather.13.cloned.1.call-start = ((), (), s32[]{:S(2)}) async-start(), calls=%async_computation.9 | async-start | bytes 3145728 | tf_op jit(solution)/shard_map/all_gather | solution.py:137
  49.5 9.7 %copy-start.28 = (s32[2,512]{1,0:T(2,128)S(1)}, s32[2,512]{1,0:T(2,128)}, u32[]{:S(2)}) copy-start(s32[2,512]{1,0:T(2,128)} %param.17) | copy-start | bytes 12292
  50.9 5.5 copy-start.26
  51.0 9.1 %copy-start.34 = (bf16[3,32]{1,0:T(4,128)(2,1)S(1)}, bf16[3,32]{1,0:T(4,128)(2,1)}, u32[]{:S(2)}) copy-start(bf16[3,32]{1,0:T(4,128)(2,1)} %param.21) | copy-start | bytes 580
  51.0 27.9 %copy-start.35 = (bf16[128]{0:T(256)(128)(2,1)S(1)}, bf16[128]{0:T(256)(128)(2,1)}, u32[]{:S(2)}) copy-start(bf16[128]{0:T(256)(128)(2,1)} %param.24) | copy-start | bytes 772
  52.6 6.5 copy-start.32
  52.6 6.5 copy-start.30
  52.7 3.8 copy-start.24
  56.5 110.8 %all-gather.15.cloned.1.call-start = ((), (), s32[]{:S(2)}) async-start(), calls=%async_computation.10 | async-start | bytes 3342336 | tf_op jit(solution)/shard_map/all_gather | solution.py:107
  57.0 312.2 %all-gather.19.cloned.1.call-start = ((), (), s32[]{:S(2)}) async-start(), calls=%async_computation.12 | async-start | bytes 3145728 | tf_op jit(solution)/shard_map/all_gather | solution.py:138
  57.6 311.6 %all-gather.21.cloned.1.call-start = ((), (), s32[]{:S(2)}) async-start(), calls=%async_computation.13 | async-start | bytes 4456448 | tf_op jit(solution)/shard_map/all_gather | solution.py:110
  58.2 321.7 %all-gather.23.cloned.1.call-start = ((), (), s32[]{:S(2)}) async-start(), calls=%async_computation.14 | async-start | bytes 4456448 | tf_op jit(solution)/shard_map/all_gather | solution.py:112
  59.0 410.2 %reduce-scatter.20.cloned.1.call-start = ((), (), s32[]{:S(2)}) async-start(), calls=%async_computation.17 | async-start | bytes 3145728 | tf_op jit(solution)/shard_map/reduce_scatter | solution.py:209
  97.5 96.7 %copy-start.18 = (f32[2,512,16]{1,0,2:T(2,128)}, f32[2,512,16]{1,0,2:T(2,128)S(1)}, u32[]{:S(2)}) copy-start(f32[2,512,16]{1,0,2:T(2,128)S(1)} %get-tuple-element.306) | copy-start | bytes 196612
  97.5 96.7 %copy-start.20 = (f32[2,512,16]{1,0,2:T(2,128)}, f32[2,512,16]{1,0,2:T(2,128)S(1)}, u32[]{:S(2)}) copy-start(f32[2,512,16]{1,0,2:T(2,128)S(1)} %get-tuple-element.307) | copy-start | bytes 196612
  173.2 4.2 copy-start.11
  187.1 3.8 copy-start.10
  221.0 3.3 copy-start
  274.7 6.6 copy-start.4
  282.6 3.3 copy-start
  336.3 6.6 copy-start.4
  369.2 100.0 %reduce-scatter.22.cloned.1.call-start = ((), (), s32[]{:S(2)}) async-start(), calls=%async_computation.18 | async-start | bytes 3145728 | tf_op jit(solution)/shard_map/reduce_scatter | solution.py:215
  369.3 10.6 %copy-start.29 = (f32[16,1,128]{2,1,0:T(1,128)S(1)}, f32[16,1,128]{2,1,0:T(1,128)}, u32[]{:S(2)}) copy-start(f32[16,1,128]{2,1,0:T(1,128)} %convert_element_type.186) | copy-start | bytes 24580
  379.9 27.9 %copy-start.37 = (bf16[1024,2048]{1,0:T(8,128)(2,1)S(1)}, bf16[1024,2048]{1,0:T(8,128)(2,1)}, u32[]{:S(2)}) copy-start(bf16[1024,2048]{1,0:T(8,128)(2,1)} %all-gather.21.cloned.1.call-done) | copy-start | bytes 12582916
  407.8 5.7 copy-start.40
  413.5 65.2 %reduce-scatter.18.cloned.1.call-start = ((), (), s32[]{:S(2)}) async-start(), calls=%async_computation.15 | async-start | bytes 3145728 | tf_op jit(solution)/shard_map/reduce_scatter | solution.py:167
  425.8 8.3 copy-start.12
  425.8 8.3 copy-start.15
  425.8 8.3 copy-start.17
  434.1 2.8 copy-start.13
  434.1 2.8 copy-start.14
  436.8 101.4 %reduce-scatter.30.cloned.1.call-start = ((), (), s32[]{:S(2)}) async-start(), calls=%async_computation.22 | async-start | bytes 139264
  438.3 160.3 %reduce-scatter.32.cloned.1.call-start = ((), (), s32[]{:S(2)}) async-start(), calls=%async_computation.23 | async-start | bytes 1114112
  443.0 7.3 copy-start.36
  443.0 26.2 %copy-start.2 = (bf16[2,256,1024]{2,1,0:T(8,128)(2,1)S(1)}, bf16[2,256,1024]{2,1,0:T(8,128)(2,1)}, u32[]{:S(2)}) copy-start(bf16[2,256,1024]{2,1,0:T(8,128)(2,1)} %param.16) | copy-start | bytes 3145732
  443.0 26.2 %copy-start.23 = (f32[1,1024]{1,0:T(1,128)S(1)}, f32[1,1024]{1,0:T(1,128)}, u32[]{:S(2)}) copy-start(f32[1,1024]{1,0:T(1,128)} %copy-done.22) | copy-start | bytes 12292
  443.0 26.2 %copy-start.25 = (f32[1,1024]{1,0:T(1,128)S(1)}, f32[1,1024]{1,0:T(1,128)}, u32[]{:S(2)}) copy-start(f32[1,1024]{1,0:T(1,128)} %copy-done.24) | copy-start | bytes 12292
  443.0 26.2 %copy-start.27 = (f32[2,256]{1,0:T(2,128)S(1)}, f32[2,256]{1,0:T(2,128)}, u32[]{:S(2)}) copy-start(f32[2,256]{1,0:T(2,128)} %copy-done.26) | copy-start | bytes 6148
  443.0 224.5 %reduce-scatter.24.cloned.1.call-start = ((), (), s32[]{:S(2)}) async-start(), calls=%async_computation.19 | async-start | bytes 3342336 | tf_op jit(solution)/shard_map/reduce_scatter | solution.py:240
  450.2 21.8 %copy-start.33 = (f32[2,256]{1,0:T(2,128)S(1)}, f32[2,256]{1,0:T(2,128)}, u32[]{:S(2)}) copy-start(f32[2,256]{1,0:T(2,128)} %copy-done.32) | copy-start | bytes 6148
  450.2 21.9 %copy-start.31 = (f32[2,256]{1,0:T(2,128)S(1)}, f32[2,256]{1,0:T(2,128)}, u32[]{:S(2)}) copy-start(f32[2,256]{1,0:T(2,128)} %copy-done.30) | copy-start | bytes 6148
  450.2 275.5 %reduce-scatter.28.cloned.1.call-start = ((), (), s32[]{:S(2)}) async-start(), calls=%async_computation.21 | async-start | bytes 278528
  469.2 9.5 %copy-start.8 = (bf16[2,256,1024]{2,1,0:T(8,128)(2,1)S(1)}, bf16[2,256,1024]{2,1,0:T(8,128)(2,1)}, u32[]{:S(2)}) copy-start(bf16[2,256,1024]{2,1,0:T(8,128)(2,1)} %reduce-scatter.20.cloned.1.call-done) | copy-start | bytes 3145732
  469.3 9.4 %copy-start.9 = (bf16[2,256,1024]{2,1,0:T(8,128)(2,1)S(1)}, bf16[2,256,1024]{2,1,0:T(8,128)(2,1)}, u32[]{:S(2)}) copy-start(bf16[2,256,1024]{2,1,0:T(8,128)(2,1)} %reduce-scatter.22.cloned.1.call-done) | copy-start | bytes 3145732
  491.2 309.7 %reduce-scatter.34.cloned.1.call-start = ((), (), s32[]{:S(2)}) async-start(), calls=%async_computation.24 | async-start | bytes 4456448
  507.3 369.4 %reduce-scatter.26.cloned.1.call-start = ((), (), s32[]{:S(2)}) async-start(), calls=%async_computation.20 | async-start | bytes 4456448 | tf_op jit(solution)/shard_map/reduce_scatter | solution.py:249
  (16 other events, 26.8 us)
Sparse Core Ops, SparseCore 0:
  10.2 40.5 all-gather.16
  52.3 32.0 all-gather.24
  86.6 33.1 all-gather.12
  121.8 45.4 all-gather.14
  168.7 31.9 all-gather.18
  202.7 50.5 all-gather.20
  255.4 49.2 all-gather.22
  369.3 31.0 reduce-scatter.19
  413.6 31.0 reduce-scatter.21
  446.8 31.8 reduce-scatter.17
  483.1 55.0 reduce-scatter.29
  542.1 56.4 reduce-scatter.31
  602.4 65.0 reduce-scatter.23
  671.5 54.2 reduce-scatter.27
  729.4 71.3 reduce-scatter.33
  805.1 71.5 reduce-scatter.25
where the time goes:
time: 900 us; the launch traced here: 885 us
  waiting for transfers between devices  386 us (43%)
  local copies, waits for them, and re-layouts  155 us (17%)
  matrix products  141 us (16%)
  blocking collectives  132 us (15%)
  other arithmetic  54.6 us (6%)
  between operations  15.9 us (2%)
    unnamed x20, waiting for transfers between devices  212 us
    dynamic_update_slice x8, local copies, waits for them, and re-layouts, on_device(): lax.map(attend_back, (queries, key_rows, value_rows, allowed, log_total,...  82.6 us
    reduce_scatter x1, waiting for transfers between devices, on_device(): lax.psum_scatter(in_weight_grad.astype(jnp.bfloat16), 'fsdp', scatter_dim...  73.6 us
    all_gather x1, waiting for transfers between devices, on_device(): lax.all_gather(qkv_weight, 'fsdp', axis=0, tiled=True)  47.5 us
    reduce_scatter x1, waiting for transfers between devices, on_device(): lax.psum_scatter(qkv_grad.astype(jnp.bfloat16), 'fsdp', scatter_dimension...  37.1 us
    unnamed x1, blocking collectives  29.5 us
    dot_general x1, matrix products, on_device(): act_grad = jnp.dot(grad_flat, out_full, preferred_element_type=jnp.float32)  27.8 us
    all_gather x1, blocking collectives, on_device(): lax.all_gather(norm_gain, 'fsdp', axis=1, tiled=True)  23.1 us
  transfers between devices with their start and end apart: 16, of which 9 were waited for; matrix products, arithmetic and copies ran while one was open for 38% of the time, Pallas kernels for 0%

commit v1 on v0

v1 whole, which is shorter than its diff:
```python
import functools
import math

import jax
import jax.numpy as jnp
from jax import lax
from jax.experimental import pallas as pl
from jax.experimental.pallas import tpu as pltpu
from jax.sharding import PartitionSpec as P

HEAD_DIM = 64
ROT_DIM = 16
PAIR = 2 * HEAD_DIM


norm_eps = 1e-05
masked_fill = -1e30


def rotary_rows(segment_rows):
    row_width = segment_rows.shape[-1]
    places = jnp.arange(row_width, dtype=jnp.int32)
    same_doc = segment_rows[..., :, None] == segment_rows[..., None, :]
    allowed = jnp.logical_and(same_doc, places[None, :] <= places[:, None])
    positions = jnp.sum(allowed.astype(jnp.int32), axis=-1) - 1
    half_dim = ROT_DIM // 2
    frequency = jnp.exp(
        jnp.arange(half_dim, dtype=jnp.float32) * (-2.0 * math.log(10000.0) / ROT_DIM)
    )
    angles = positions.astype(jnp.float32)[..., None] * frequency
    cosine, sine = jnp.cos(angles), jnp.sin(angles)
    rest = HEAD_DIM - ROT_DIM
    ones = jnp.ones(angles.shape[:-1] + (rest,), jnp.float32)
    blank = jnp.zeros_like(ones)
    half_blank = jnp.zeros_like(sine)
    keep = jnp.concatenate([cosine, cosine, ones], axis=-1)
    ahead = jnp.concatenate([-sine, half_blank, blank], axis=-1)
    behind = jnp.concatenate([half_blank, sine, blank], axis=-1)
    return tuple(jnp.concatenate([part, part], axis=-1) for part in (keep, ahead, behind))


def attention_kernel(
    seg_row, seg_col, keep, ahead, behind, proj, mixed_grad, mixed_out, grad_out
):
    half_dim = ROT_DIM // 2
    scale = HEAD_DIM ** (-0.5)
    c, a, b = keep[0], ahead[0], behind[0]

    def turn(u):
        return u * c + pltpu.roll(u, PAIR - half_dim, 1) * a + pltpu.roll(u, half_dim, 1) * b

    def turn_back(w):
        return w * c - pltpu.roll(w, PAIR - half_dim, 1) * a - pltpu.roll(w, half_dim, 1) * b

    def dot(x, y, dims):
        return lax.dot_general(x, y, (dims, ((), ())), preferred_element_type=jnp.float32)

    queries = turn(proj[0]).astype(jnp.bfloat16)
    key_rows = turn(proj[1]).astype(jnp.bfloat16)
    value_rows = proj[2].astype(jnp.bfloat16)
    d_mixed = mixed_grad[...]
    row_len = queries.shape[0]
    lane = lax.broadcasted_iota(jnp.int32, (row_len, PAIR), 1)
    first = lane < HEAD_DIM
    q_place = lax.broadcasted_iota(jnp.int32, (row_len, row_len), 0)
    k_place = lax.broadcasted_iota(jnp.int32, (row_len, row_len), 1)
    allowed = jnp.logical_and(seg_row[0] == seg_col[0], k_place <= q_place)
    results = []
    for head in range(2):
        mine = first if head == 0 else jnp.logical_not(first)
        q_head = jnp.where(mine, queries, jnp.zeros_like(queries))
        d_head = jnp.where(mine, d_mixed, jnp.zeros_like(d_mixed))
        scores = dot(q_head, key_rows, ((1,), (1,))) * scale
        masked = jnp.where(allowed, scores, masked_fill)
        largest = jnp.max(masked, axis=-1, keepdims=True)
        expanded = jnp.exp(masked - largest)
        summed = jnp.sum(expanded, axis=-1, keepdims=True)
        weights = expanded * (1.0 / summed)
        low = weights.astype(jnp.bfloat16)
        mixed = dot(low, value_rows, ((1,), (0,)))
        weight_grad = dot(d_head, value_rows, ((1,), (1,)))
        inner = jnp.sum(weights * weight_grad, axis=-1, keepdims=True)
        score_grad = (weights * (weight_grad - inner)).astype(jnp.bfloat16)
        value_grad = dot(low, d_mixed, ((0,), (0,)))
        query_grad = dot(score_grad, key_rows, ((1,), (0,))) * scale
        key_grad = dot(score_grad, queries, ((0,), (0,))) * scale
        results.append((mixed, query_grad, key_grad, value_grad))
    mixed, query_grad, key_grad, value_grad = [
        jnp.where(first, one, two) for one, two in zip(*results)
    ]
    mixed_out[...] = mixed.astype(mixed_out.dtype)
    grad_out[0] = turn_back(query_grad).astype(grad_out.dtype)
    grad_out[1] = turn_back(key_grad).astype(grad_out.dtype)
    grad_out[2] = value_grad.astype(grad_out.dtype)


def attention(segment_ids, tables, proj, mixed_grad):
    seq_count, row_len = segment_ids.shape
    _, token_count, width = proj.shape
    pairs = width // PAIR
    table_spec = pl.BlockSpec((1, row_len, PAIR), lambda s, h: (s, 0, 0))
    flat_spec = pl.BlockSpec((row_len, PAIR), lambda s, h: (s, h))
    three_spec = pl.BlockSpec((3, row_len, PAIR), lambda s, h: (0, s, h))
    cells = seq_count * pairs * 2 * row_len * row_len
    return pl.pallas_call(
        attention_kernel,
        grid=(seq_count, pairs),
        in_specs=[
            pl.BlockSpec((1, 1, row_len), lambda s, h: (s, 0, 0)),
            pl.BlockSpec((1, row_len, 1), lambda s, h: (s, 0, 0)),
            table_spec,
            table_spec,
            table_spec,
            three_spec,
            flat_spec,
        ],
        out_specs=[flat_spec, three_spec],
        out_shape=[
            jax.ShapeDtypeStruct((token_count, width), jnp.bfloat16),
            jax.ShapeDtypeStruct((3, token_count, width), jnp.bfloat16),
        ],
        compiler_params=pltpu.CompilerParams(vmem_limit_bytes=40 * 2**20),
        cost_estimate=pl.CostEstimate(
            flops=cells * 12 * PAIR, bytes_accessed=proj.size * 8, transcendentals=cells
        ),
    )(segment_ids[:, None, :], segment_ids[:, :, None], *tables, proj, mixed_grad)


def join_rows(local, parts):
    if parts != 2:
        return lax.all_gather(local, "tp", axis=1, tiled=True)
    other = lax.ppermute(local, "tp", [(0, 1), (1, 0)])
    upper = lax.axis_index("tp") == 0
    return jnp.concatenate(
        [jnp.where(upper, local, other), jnp.where(upper, other, local)], axis=1
    )


def share_rows(partial, parts):
    if parts != 2:
        return lax.psum_scatter(
            partial.astype(jnp.bfloat16), "tp", scatter_dimension=1, tiled=True
        ).astype(jnp.float32)
    half = partial.shape[1] // 2
    mine = lax.axis_index("tp")
    away = lax.dynamic_slice_in_dim(partial, (1 - mine) * half, half, 1).astype(jnp.bfloat16)
    arrived = lax.ppermute(away, "tp", [(0, 1), (1, 0)])
    return lax.dynamic_slice_in_dim(partial, mine * half, half, 1) + arrived.astype(jnp.float32)


def pad_rows(values, width):
    groups, count = values.shape
    rows = -(-count // width)
    rows = -(-rows // 16) * 16
    return jnp.pad(values, ((0, 0), (0, rows * width - count))).reshape(groups, rows, width)


def on_device(
    shards,
    parts,
    hidden_in,
    segment_ids,
    norm_gain,
    norm_bias,
    qkv_weight,
    qkv_bias,
    dense_weight,
    mlp_in_weight,
    mlp_in_bias,
    mlp_out_weight,
    out_bias,
    out_grad,
):
    f32, bf16 = jnp.float32, jnp.bfloat16
    seq_count, local_len, model_width = hidden_in.shape
    row_len = segment_ids.shape[1]
    token_count = seq_count * row_len
    own_rows, _, local_width = qkv_weight.shape
    hidden = mlp_in_weight.shape[1]
    own_features = norm_gain.shape[1]
    own_bias, own_hidden = qkv_bias.shape[1], mlp_in_bias.shape[0]

    small = jnp.concatenate(
        [norm_gain.ravel(), norm_bias.ravel(), out_bias.ravel(), qkv_bias.ravel(), mlp_in_bias]
    )
    small_rows = pad_rows(small[None], hidden)[0]
    mlp_pack = lax.all_gather(
        jnp.concatenate([mlp_in_weight, mlp_out_weight, small_rows], axis=0), "fsdp", axis=0
    )
    rows = join_rows(hidden_in, parts).reshape(token_count, model_width).astype(f32)
    grad_flat = join_rows(out_grad, parts).reshape(token_count, model_width)
    attn_local = jnp.concatenate(
        [qkv_weight[:, 0], qkv_weight[:, 1], qkv_weight[:, 2], dense_weight], axis=0
    )
    mlp_pack, attn_local = lax.optimization_barrier((mlp_pack, attn_local))
    attn_pack = lax.all_gather(attn_local, "fsdp", axis=0)

    in_full = mlp_pack[:, :own_rows].reshape(model_width, hidden)
    out_full = mlp_pack[:, own_rows : 2 * own_rows].reshape(model_width, hidden)
    small_all = mlp_pack[:, 2 * own_rows :].reshape(shards, -1).astype(f32)
    features = small_all[:, : 6 * own_features].reshape(shards, 6, own_features)
    features = features.transpose(1, 0, 2).reshape(6, model_width)
    gains, shifts, out_shift = features[0:2], features[2:4], features[4:6]
    at = 6 * own_features
    qkv_shift = small_all[:, at : at + 3 * own_bias].reshape(shards, 3, own_bias)
    qkv_shift = qkv_shift.transpose(1, 0, 2).reshape(3, local_width)
    at = at + 3 * own_bias
    in_shift = small_all[:, at : at + own_hidden].reshape(hidden)

    centered = rows - jnp.mean(rows, axis=-1, keepdims=True)
    spread = lax.rsqrt(jnp.mean(centered * centered, axis=-1, keepdims=True) + norm_eps)
    xhat = centered * spread
    attn_flat = (xhat * gains[0] + shifts[0]).astype(bf16)
    mlp_flat = (xhat * gains[1] + shifts[1]).astype(bf16)

    pre_act = jnp.dot(mlp_flat, in_full, preferred_element_type=f32) + in_shift
    share = 0.5 * (1.0 + lax.erf(pre_act * math.sqrt(0.5)))
    act_low = (pre_act * share).astype(bf16)
    slope = (
        share + pre_act * jnp.exp(-0.5 * pre_act * pre_act) * (1.0 / math.sqrt(2.0 * math.pi))
    ).astype(bf16)
    act_grad = jnp.dot(grad_flat, out_full, preferred_element_type=f32)
    pre_grad = (act_grad * slope.astype(f32)).astype(bf16)
    in_weight_grad = jnp.einsum("nd,nf->df", mlp_flat, pre_grad, preferred_element_type=f32)
    out_weight_grad = jnp.einsum("nd,nf->df", grad_flat, act_low, preferred_element_type=f32)
    mlp_grads = jnp.concatenate(
        [
            in_weight_grad.astype(bf16).reshape(shards, own_rows, hidden),
            out_weight_grad.astype(bf16).reshape(shards, own_rows, hidden),
        ],
        axis=1,
    )
    mlp_grads, attn_pack = lax.optimization_barrier((mlp_grads, attn_pack))
    mlp_owned = lax.psum_scatter(mlp_grads, "fsdp", scatter_dimension=0, tiled=False)

    attn_parts = attn_pack.reshape(shards, 4, own_rows, local_width).transpose(1, 0, 2, 3)
    attn_parts = attn_parts.reshape(4, model_width, local_width)
    qkv_full, dense_full = attn_parts[0:3], attn_parts[3]
    proj = (
        jnp.einsum("nd,jde->jne", attn_flat, qkv_full, preferred_element_type=f32)
        + qkv_shift[:, None, :]
    )
    mixed_grad = jnp.dot(grad_flat, dense_full, preferred_element_type=f32).astype(bf16)
    mixed_flat, proj_grad = attention(segment_ids, rotary_rows(segment_ids), proj, mixed_grad)

    qkv_grad = jnp.einsum("nd,jne->jde", attn_flat, proj_grad, preferred_element_type=f32)
    dense_grad = jnp.einsum("nd,ne->de", grad_flat, mixed_flat, preferred_element_type=f32)
    attn_input_grad = jnp.einsum("jne,jde->nd", proj_grad, qkv_full, preferred_element_type=f32)
    mlp_input_grad = jnp.einsum("nf,df->nd", pre_grad, in_full, preferred_element_type=f32)
    normed_grad = (attn_input_grad * gains[0] + mlp_input_grad * gains[1]).reshape(
        seq_count, row_len, model_width
    )
    normed_grad = share_rows(normed_grad, parts)
    vectors = jnp.stack(
        [
            jnp.sum(attn_input_grad * xhat, axis=0),
            jnp.sum(mlp_input_grad * xhat, axis=0),
            jnp.sum(attn_input_grad, axis=0),
            jnp.sum(mlp_input_grad, axis=0),
            jnp.sum(out_grad.astype(f32), axis=(0, 1)),
        ]
    )
    if parts == 2:
        vectors = vectors + lax.ppermute(vectors, "tp", [(0, 1), (1, 0)])
    else:
        vectors = lax.psum(vectors, "tp")
    qkv_bias_grad = jnp.sum(proj_grad.astype(f32), axis=1)
    in_bias_grad = jnp.sum(pre_grad.astype(f32), axis=0)
    small_grads = jnp.concatenate(
        [
            vectors.reshape(5, shards, own_features).transpose(1, 0, 2).reshape(shards, -1),
            qkv_bias_grad.reshape(3, shards, own_bias).transpose(1, 0, 2).reshape(shards, -1),
            in_bias_grad.reshape(shards, own_hidden),
        ],
        axis=1,
    ).astype(bf16)
    attn_grads = jnp.concatenate(
        [qkv_grad[j].astype(bf16).reshape(shards, own_rows, local_width) for j in range(3)]
        + [dense_grad.astype(bf16).reshape(shards, own_rows, local_width)]
        + [pad_rows(small_grads, local_width)],
        axis=1,
    )
    attn_owned = lax.psum_scatter(attn_grads, "fsdp", scatter_dimension=0, tiled=False)

    attn_part = jnp.einsum("ne,de->nd", mixed_flat, dense_full, preferred_element_type=f32)
    mlp_part = jnp.einsum("nf,df->nd", act_low, out_full, preferred_element_type=f32)
    branches = share_rows((attn_part + mlp_part).reshape(seq_count, row_len, model_width), parts)
    local_rows = hidden_in.astype(f32)
    hidden_out = (local_rows + branches + out_shift[0] + out_shift[1]).astype(bf16)

    local_centered = local_rows - jnp.mean(local_rows, axis=-1, keepdims=True)
    local_spread = lax.rsqrt(
        jnp.mean(local_centered * local_centered, axis=-1, keepdims=True) + norm_eps
    )
    local_hat = local_centered * local_spread
    inner = jnp.mean(normed_grad * local_hat, axis=-1, keepdims=True)
    level = jnp.mean(normed_grad, axis=-1, keepdims=True)
    input_grad = out_grad.astype(f32) + (normed_grad - level - local_hat * inner) * local_spread

    owned = attn_owned[: 4 * own_rows].astype(f32).reshape(4, own_rows, local_width)
    small_owned = attn_owned[4 * own_rows :].astype(f32).ravel()
    vector_owned = small_owned[: 5 * own_features].reshape(5, own_features)
    at = 5 * own_features
    bias_owned = small_owned[at : at + 3 * own_bias].reshape(3, own_bias)
    at = at + 3 * own_bias
    hidden_owned = small_owned[at : at + own_hidden]
    return (
        hidden_out,
        input_grad,
        vector_owned[0:2],
        vector_owned[2:4],
        owned[0:3].transpose(1, 0, 2),
        bias_owned,
        owned[3],
        mlp_owned[:own_rows].astype(f32),
        hidden_owned,
        mlp_owned[own_rows:].astype(f32),
        jnp.stack([vector_owned[4], vector_owned[4]]),
    )


def solution(mesh):
    in_specs = (
        P("fsdp", "tp", None),
        P("fsdp", None),
        P(None, "fsdp"),
        P(None, "fsdp"),
        P("fsdp", None, "tp"),
        P(None, ("tp", "fsdp")),
        P("fsdp", "tp"),
        P("fsdp", "tp"),
        P(("tp", "fsdp")),
        P("fsdp", "tp"),
        P(None, "fsdp"),
        P("fsdp", "tp", None),
    )
    out_specs = (
        P("fsdp", "tp", None),
        P("fsdp", "tp", None),
        P(None, "fsdp"),
        P(None, "fsdp"),
        P("fsdp", None, "tp"),
        P(None, ("tp", "fsdp")),
        P("fsdp", "tp"),
        P("fsdp", "tp"),
        P(("tp", "fsdp")),
        P("fsdp", "tp"),
        P(None, "fsdp"),
    )
    return jax.shard_map(
        functools.partial(on_device, mesh.shape["fsdp"], mesh.shape["tp"]),
        mesh=mesh,
        in_specs=in_specs,
        out_specs=out_specs,
        check_vma=False,
    )
```

time: 900 us -> 464 us (0.52)
  blocking collectives: 132 us -> 0 us
  waiting for transfers between devices: 386 us -> 262 us
  local copies, waits for them, and re-layouts: 155 us -> 45.6 us
  matrix products: 141 us -> 67.4 us
  Pallas kernels: 0 us -> 25.1 us
  other arithmetic: 54.6 us -> 36 us
    unnamed x20 -> x4, waiting for transfers between devices: 212 us -> 0.57 us
    all_gather x5 -> x0, blocking collectives: 95.5 us -> none  [the longest x1 23.1 us: on_device(): lax.all_gather(norm_gain, 'fsdp', axis=1, tiled=True)]
    dynamic_update_slice x8 -> x0, local copies, waits for them, and re-layouts: 82.6 us -> none  [on_device(): lax.map(attend_back, (queries, key_rows, value_rows, allowed, log_total,...]
    dot_general x26 -> x12, matrix products: 141 us -> 67.4 us  [the longest x1 9.96 us: on_device(): jnp.einsum('nf,df->nd', act_low, out_full, preferred_element_type=f32)]
    reduce_scatter x5 -> x2, waiting for transfers between devices: 114 us -> 174 us  [the longest x1 103 us: on_device(): lax.psum_scatter(mlp_grads, 'fsdp', scatter_dimension=0, tiled=False)]
    ppermute x0 -> x5, waiting for transfers between devices: none -> 56.7 us  [the longest x2 33.3 us: join_rows(): other = lax.ppermute(local, 'tp', [(0, 1), (1, 0)])]
    all_gather x7 -> x2, waiting for transfers between devices: 60.7 us -> 30.4 us  [the longest x1 30.4 us: on_device(): lax.all_gather(jnp.concatenate([mlp_in_weight, mlp_out_weight, small_rows...]
    unnamed x1 -> x0, blocking collectives: 29.5 us -> none
  transfers between devices with their start and end apart: 16 -> 9, of which waited for: 9 -> 7; matrix products, arithmetic and copies ran while one was open for 38% -> 23% of each run, Pallas kernels for 0% -> 0%
where the time goes in v1:
time: 464 us; the launch traced here: 457 us
  waiting for transfers between devices  262 us (56%)
  matrix products  67.4 us (15%)
  local copies, waits for them, and re-layouts  45.6 us (10%)
  other arithmetic  36 us (8%)
  Pallas kernels  25.1 us (5%)
  between operations  14.7 us (3%)
  starting transfers between devices  7.05 us (2%)
    reduce_scatter x1, waiting for transfers between devices, on_device(): lax.psum_scatter(mlp_grads, 'fsdp', scatter_dimension=0, tiled=False)  103 us
    reduce_scatter x1, waiting for transfers between devices, on_device(): lax.psum_scatter(attn_grads, 'fsdp', scatter_dimension=0, tiled=False)  71.3 us
    ppermute x2, waiting for transfers between devices, join_rows(): other = lax.ppermute(local, 'tp', [(0, 1), (1, 0)])  33.3 us
    all_gather x1, waiting for transfers between devices, on_device(): lax.all_gather(jnp.concatenate([mlp_in_weight, mlp_out_weight, small_rows...  30.4 us
    pallas_call x1, Pallas kernels, attention(): pl.pallas_call(attention_kernel, grid=(seq_count, pairs), in_specs=[pl.Bl...  25.1 us
    ppermute x2, waiting for transfers between devices, share_rows(): arrived = lax.ppermute(away, 'tp', [(0, 1), (1, 0)])  23.3 us
    unnamed x71, local copies, waits for them, and re-layouts  11.1 us
    dot_general x1, matrix products, on_device(): jnp.einsum('nf,df->nd', act_low, out_full, preferred_element_type=f32)  9.96 us
  transfers between devices with their start and end apart: 9, of which 7 were waited for; matrix products, arithmetic and copies ran while one was open for 23% of the time, Pallas kernels for 0%

profile of v1, /device:TPU:0, one launch (start us, length us, event | category | flops | bytes accessed | tf_op | source)
XLA Modules:
  0.0 457.3 jit_solution(8919606050177857101)
XLA Ops:
  11.1 1.9 pad_maximum_fusion.3
  13.1 3.0 collective-permute-start.1
  16.9 1.7 copy.54.seg_col
  18.7 1.4 convert_reduce_fusion.3
  20.1 1.9 multiply_sine_fusion
  22.1 1.7 concatenate.42.behind
  23.8 1.7 concatenate.41.ahead
  25.6 1.7 concatenate.40.keep
  28.7 11.7 %collective-permute-done.1 = bf16[2,256,1024]{2,1,0:T(8,128)(2,1)} collective-permute-done((bf16[2,256,1024]{2,1,0:T(8,128)(2,1)}, bf16[2,256,1024]{2,1,0:T(8,128)(2,1)}, u32[]{:S(2)}, u32[]{:S(2)}) %collective-permute-start.1) | collective-permute-done | bytes 1048608 | tf_op jit(solution)/shard_map/ppermute | solution.py:132
  40.4 21.6 %collective-permute-done = bf16[2,256,1024]{2,1,0:T(8,128)(2,1)} collective-permute-done((bf16[2,256,1024]{2,1,0:T(8,128)(2,1)}, bf16[2,256,1024]{2,1,0:T(8,128)(2,1)}, u32[]{:S(2)}, u32[]{:S(2)}) %collective-permute-start) | collective-permute-done | bytes 1048608 | tf_op jit(solution)/shard_map/ppermute | solution.py:132
  62.1 2.3 broadcast_select_fusion.1
  65.5 1.5 pad_maximum_fusion.2
  66.9 30.4 %all-gather.5.cloned.1.call-done = bf16[2304,2048]{1,0:T(8,128)(2,1)} async-done(((bf16[144,2048]{1,0:T(8,128)(2,1)}), bf16[2304,2048]{1,0:T(8,128)(2,1)}) %all-gather.5.cloned.1.call-update) | async-done | bytes 9437200 | tf_op jit(solution)/shard_map/all_gather | solution.py:187
  97.6 1.5 slice_convert_fusion
  100.3 1.3 copy-done.23
  105.0 2.3 add_convert_fusion.1
  107.3 1.2 copy-done.13
  109.8 7.4 %multiply_convert_fusion = (bf16[1024,2048]{1,0:T(8,128)(2,1)S(1)}, f32[1024,2048]{1,0:T(8,128)}) fusion(f32[2048]{0:T(1024)S(1)} %slice_bitcast_fusion.6, bf16[1024,1024]{1,0:T(8,128)(2,1)S(1)} %bitcast.152, bf16[1024,2048]{1,0:T(8,128)(2,1)S(1)} %bitcast.136), kind=kOutput, calls=%fused_computation.7 | convolution fusion | flops 4307550208 | bytes 18882560 | tf_op jit(solution)/shard_map/dot_general | solution.py:216
  117.2 6.3 %convolution_convert_fusion = bf16[1024,2048]{1,0:T(8,128)(2,1)} fusion(bf16[1024,1024]{1,0:T(8,128)(2,1)S(1)} %bitcast.147, bf16[1024,2048]{1,0:T(8,128)(2,1)S(1)} %get-tuple-element.70), kind=kOutput, calls=%fused_computation.24 | convolution fusion | flops 4297064448 | bytes 10485760 | tf_op jit(solution)/shard_map/nd,nf->df/dot_general | solution.py:225
  123.5 9.3 %fusion.35 = (bf16[2048]{0:T(1024)(128)(2,1)S(1)}, bf16[1024,2048]{1,0:T(8,128)(2,1)S(1)}) fusion(f32[1024,2048]{1,0:T(8,128)} %get-tuple-element.71, f32[2048]{0:T(1024)S(1)} %slice_bitcast_fusion.6, bf16[1024,1024]{1,0:T(8,128)(2,1)S(1)} %bitcast.148, bf16[1024,2048]{1,0:T(8,128)(2,1)S(1)} %bitcast.138), kind=kOutput, calls=%fused_computation.114 | convolution fusion | flops 4324325376 | bytes 18886656 | tf_op jit(solution)/shard_map/dot_general | solution.py:222
  132.8 6.6 %convolution_convert_fusion.1 = bf16[1024,2048]{1,0:T(8,128)(2,1)} fusion(bf16[1024,1024]{1,0:T(8,128)(2,1)S(1)} %add_convert_fusion.3, bf16[1024,2048]{1,0:T(8,128)(2,1)S(1)} %get-tuple-element.73), kind=kOutput, calls=%fused_computation.25 | convolution fusion | flops 4297064448 | bytes 10485760 | tf_op jit(solution)/shard_map/nd,nf->df/dot_general | solution.py:224
  139.4 8.4 %pad_maximum_fusion = bf16[16,128,2048]{2,1,0:T(8,128)(2,1)} fusion(bf16[16,64,2048]{2,1,0:T(8,128)(2,1)} %bitcast.140, bf16[16,64,2048]{2,1,0:T(8,128)(2,1)} %bitcast.141), kind=kLoop, calls=%fused_computation.6 | loop fusion | flops 16777216 | bytes 16777216 | tf_op jit(solution)/shard_map/concatenate | solution.py:226
  147.8 10.0 %fusion.36 = f32[1024,1024]{1,0:T(8,128)} fusion(bf16[1024,2048]{1,0:T(8,128)(2,1)} %copy-done.30, bf16[1024,2048]{1,0:T(8,128)(2,1)} %bitcast.139), kind=kOutput, calls=%fused_computation.115 | convolution fusion | flops 4294967296 | bytes 12582912 | tf_op jit(solution)/shard_map/nf,df->nd/dot_general | solution.py:286
  157.8 1.3 slice.200
  159.1 2.2 slice.198
  163.1 3.4 add_bitcast_fusion.proj
  166.6 25.1 %shard_map.203 = (bf16[1024,512]{1,0:T(8,128)(2,1)S(1)}, bf16[3,1024,512]{2,1,0:T(8,128)(2,1)S(1)}) custom-call(s32[2,1,512]{2,1,0:T(1,128)S(1)} %broadcast_in_dim.12.seg_row, s32[2,512,1]{2,1,0:T(8,128)S(1)} %copy-done.5, f32[2,512,128]{2,1,0:T(8,128)S(1)} %copy-done.4, f32[2,512,128]{2,1,0:T(8,128)S(1)} %copy-done.3, f32[2,512,128]{2,1,0:T(8,128)S(1)} %copy-done.2, ...), custom_call_target="tpu_custom_call" | custom-call | flops 6442450944 | bytes 12582912 | tf_op jit(solution)/shard_map/pallas_call | solution.py:105
  191.7 5.0 %fusion.37 = f32[1024,1024,1]{1,0,2:T(8,128)} fusion(bf16[3,1024,512]{2,1,0:T(8,128)(2,1)S(1)} %get-tuple-element.21, bf16[3,1024,512]{2,1,0:T(8,128)(2,1)S(1)} %bitcast.143), kind=kOutput, calls=%fused_computation.116 | convolution fusion | flops 3221225472 | bytes 10485760 | tf_op jit(solution)/shard_map/jne,jde->nd/dot_general | solution.py:248
  196.7 9.0 %fusion.31 = (f32[1024]{0:T(1024)S(1)}, f32[1024]{0:T(1024)S(1)}, f32[1024,1024]{1,0:T(8,128)S(1)}, f32[1024]{0:T(1024)S(1)}, f32[1024]{0:T(1024)S(1)}, /*index=5*/bf16[1024,1024]{1,0:T(8,128)(2,1)S(1)}) fusion(f32[1024]{0:T(1024)S(1)} %bitcast.168, f32[1024]{0:T(1024)S(1)} %bitcast.166, bf16[2,256,1024]{2,1,0:T(8,128)(2,1)S(1)} %copy-done.9, ...), kind=kOutput, calls=%fused_computation.110 | convolution fusion | flops 4313837568 | bytes 21008384 | tf_op jit(solution)/shard_map/nf,df->nd/dot_general | solution.py:249
  205.7 3.7 convert_bitcast_fusion
  210.6 1.5 collective-permute-start.3
  212.1 3.2 convolution_add_fusion
  215.3 1.8 fusion.33
  217.1 2.3 copy.58
  219.4 2.3 copy.57
  221.6 2.3 copy.56
  223.9 1.9 dynamic-slice_convert_fusion.1
  226.5 2.3 constant_dynamic-update-slice_fusion.4
  230.9 2.3 convolution_convert_fusion.2
  233.2 3.7 collective-permute-done.3
  236.9 2.0 fusion.20
  239.0 19.6 %collective-permute-done.2 = bf16[2,256,1024]{2,1,0:T(8,128)(2,1)S(1)} collective-permute-done((bf16[2,256,1024]{2,1,0:T(8,128)(2,1)S(1)}, bf16[2,256,1024]{2,1,0:T(8,128)(2,1)S(1)}, u32[]{:S(2)}, u32[]{:S(2)}) %collective-permute-start.2) | collective-permute-done | bytes 1048608 | tf_op jit(solution)/shard_map/ppermute | solution.py:147
  258.6 3.8 convert_reduce_fusion.2
  262.4 1.5 collective-permute-start.4
  263.9 2.3 constant_dynamic-update-slice_fusion.1
  268.7 71.3 %reduce-scatter.3.cloned.1.call-done = bf16[1,272,512]{2,1,0:T(8,128)(2,1)} async-done(((bf16[16,272,512]{2,1,0:T(8,128)(2,1)}), bf16[1,272,512]{2,1,0:T(8,128)(2,1)}) %reduce-scatter.3.cloned.1.call-update) | async-done | bytes 278544 | tf_op jit(solution)/shard_map/reduce_scatter | solution.py:283
  345.6 102.6 %reduce-scatter.5.cloned.1.call-done = bf16[1,128,2048]{2,1,0:T(8,128)(2,1)} async-done(((bf16[16,128,2048]{2,1,0:T(8,128)(2,1)}), bf16[1,128,2048]{2,1,0:T(8,128)(2,1)}) %reduce-scatter.5.cloned.1.call-update) | async-done | bytes 524304 | tf_op jit(solution)/shard_map/reduce_scatter | solution.py:234
  448.3 2.1 fusion.26
  (147 shorter events, 27.4 us)
Async XLA Ops:
  7.2 90.2 %all-gather.5.cloned.1.call-start = ((), (), s32[]{:S(2)}) async-start(), calls=%async_computation.4 | async-start | bytes 10027008 | tf_op jit(solution)/shard_map/all_gather | solution.py:187
  13.0 144.7 %all-gather.7.cloned.1.call-start = ((), (), s32[]{:S(2)}) async-start(), calls=%async_computation.5 | async-start | bytes 4456448 | tf_op jit(solution)/shard_map/all_gather | solution.py:196
  13.1 27.3 %collective-permute-start.1 = (bf16[2,256,1024]{2,1,0:T(8,128)(2,1)}, bf16[2,256,1024]{2,1,0:T(8,128)(2,1)}, u32[]{:S(2)}, u32[]{:S(2)}) collective-permute-start(bf16[2,256,1024]{2,1,0:T(8,128)(2,1)} %param.23), channel_id=1, source_target_pairs={{0,1},{1,0},{2,3},{3,2},{4,5},{5,4},{6,7},{7,6},{8,9},{9,8},{10,11... | collective-permute-start | bytes 3145736 | tf_op jit(solution)/shard_map/ppermute | solution.py:132
  16.1 45.9 %collective-permute-start = (bf16[2,256,1024]{2,1,0:T(8,128)(2,1)}, bf16[2,256,1024]{2,1,0:T(8,128)(2,1)}, u32[]{:S(2)}, u32[]{:S(2)}) collective-permute-start(bf16[2,256,1024]{2,1,0:T(8,128)(2,1)} %param.12), channel_id=1, source_target_pairs={{0,1},{1,0},{2,3},{3,2},{4,5},{5,4},{6,7},{7,6},{8,9},{9,8},{10,11... | collective-permute-start | bytes 3145736 | tf_op jit(solution)/shard_map/ppermute | solution.py:132
  23.8 3.5 copy-start.27
  23.8 3.6 copy-start.28
  23.8 4.3 copy-start.6
  64.3 40.7 %copy-start.8 = (bf16[2,256,1024]{2,1,0:T(8,128)(2,1)}, bf16[2,256,1024]{2,1,0:T(8,128)(2,1)S(1)}, u32[]{:S(2)}) copy-start(bf16[2,256,1024]{2,1,0:T(8,128)(2,1)S(1)} %get-tuple-element.74) | copy-start | bytes 3145732
  64.4 40.7 %copy-start.10 = (bf16[2,256,1024]{2,1,0:T(8,128)(2,1)}, bf16[2,256,1024]{2,1,0:T(8,128)(2,1)S(1)}, u32[]{:S(2)}) copy-start(bf16[2,256,1024]{2,1,0:T(8,128)(2,1)S(1)} %get-tuple-element.75) | copy-start | bytes 3145732
  97.4 242.6 %reduce-scatter.3.cloned.1.call-start = ((), (), s32[]{:S(2)}) async-start(), calls=%async_computation.2 | async-start | bytes 4734976 | tf_op jit(solution)/shard_map/reduce_scatter | solution.py:283
  100.3 1.3 copy-start.23
  103.9 4.6 %copy-start.13 = (bf16[2304,2048]{1,0:T(8,128)(2,1)S(1)}, bf16[2304,2048]{1,0:T(8,128)(2,1)}, u32[]{:S(2)}) copy-start(bf16[2304,2048]{1,0:T(8,128)(2,1)} %all-gather.5.cloned.1.call-done) | copy-start | bytes 28311556
  109.7 7.4 %copy-start.19 = (bf16[16,64,2048]{2,1,0:T(8,128)(2,1)}, bf16[16,64,2048]{2,1,0:T(8,128)(2,1)S(1)}, u32[]{:S(2)}) copy-start(bf16[16,64,2048]{2,1,0:T(8,128)(2,1)S(1)} %get-tuple-element.36) | copy-start | bytes 12582916
  109.8 13.7 %copy-start.21 = (bf16[16,64,2048]{2,1,0:T(8,128)(2,1)}, bf16[16,64,2048]{2,1,0:T(8,128)(2,1)S(1)}, u32[]{:S(2)}) copy-start(bf16[16,64,2048]{2,1,0:T(8,128)(2,1)S(1)} %get-tuple-element.35) | copy-start | bytes 12582916
  109.8 7.4 %copy-start.24 = (bf16[2,512,1024]{2,1,0:T(8,128)(2,1)S(1)}, bf16[2,512,1024]{2,1,0:T(8,128)(2,1)}, u32[]{:S(2)}) copy-start(bf16[2,512,1024]{2,1,0:T(8,128)(2,1)} %pad_maximum_fusion.2) | copy-start | bytes 6291460
  117.2 6.3 %copy-start.30 = (bf16[1024,2048]{1,0:T(8,128)(2,1)}, bf16[1024,2048]{1,0:T(8,128)(2,1)S(1)}, u32[]{:S(2)}) copy-start(bf16[1024,2048]{1,0:T(8,128)(2,1)S(1)} %get-tuple-element.70) | copy-start | bytes 12582916
  132.8 6.6 %copy-start.29 = (bf16[1024,2048]{1,0:T(8,128)(2,1)}, bf16[1024,2048]{1,0:T(8,128)(2,1)S(1)}, u32[]{:S(2)}) copy-start(bf16[1024,2048]{1,0:T(8,128)(2,1)S(1)} %get-tuple-element.73) | copy-start | bytes 12582916
  161.5 1.6 copy-start.26
  163.1 3.4 copy-start.2
  163.1 3.4 copy-start.3
  163.1 3.5 copy-start.4
  163.1 3.5 copy-start.5
  191.7 20.4 %copy-start = (bf16[1024,512]{1,0:T(8,128)(2,1)}, bf16[1024,512]{1,0:T(8,128)(2,1)S(1)}, u32[]{:S(2)}) copy-start(bf16[1024,512]{1,0:T(8,128)(2,1)S(1)} %get-tuple-element.20) | copy-start | bytes 3145732
  191.7 5.1 %copy-start.9 = (bf16[2,256,1024]{2,1,0:T(8,128)(2,1)S(1)}, bf16[2,256,1024]{2,1,0:T(8,128)(2,1)}, u32[]{:S(2)}) copy-start(bf16[2,256,1024]{2,1,0:T(8,128)(2,1)} %copy-done.8) | copy-start | bytes 3145732
  191.7 5.0 %copy-start.11 = (bf16[2,256,1024]{2,1,0:T(8,128)(2,1)S(1)}, bf16[2,256,1024]{2,1,0:T(8,128)(2,1)}, u32[]{:S(2)}) copy-start(bf16[2,256,1024]{2,1,0:T(8,128)(2,1)} %copy-done.10) | copy-start | bytes 3145732
  191.7 5.0 %copy-start.20 = (bf16[16,64,2048]{2,1,0:T(8,128)(2,1)S(1)}, bf16[16,64,2048]{2,1,0:T(8,128)(2,1)}, u32[]{:S(2)}) copy-start(bf16[16,64,2048]{2,1,0:T(8,128)(2,1)} %copy-done.19) | copy-start | bytes 12582916
  205.7 3.8 copy-start.14
  205.7 6.4 %copy-start.16 = (f32[1024,1024]{1,0:T(8,128)S(1)}, f32[1024,1024]{1,0:T(8,128)}, u32[]{:S(2)}) copy-start(f32[1024,1024]{1,0:T(8,128)} %fusion.36) | copy-start | bytes 12582916
  210.6 26.3 %collective-permute-start.3 = (bf16[2,256,1024]{2,1,0:T(8,128)(2,1)}, bf16[2,256,1024]{2,1,0:T(8,128)(2,1)}, u32[]{:S(2)}, u32[]{:S(2)}) collective-permute-start(bf16[2,256,1024]{2,1,0:T(8,128)(2,1)} %dynamic-slice_convert_fusion), channel_id=1, source_target_pairs={{0,1},{1,0},{2,3},{3,2},{4,5},{5,4},{6,7},{7,6},{8,9},{9,8},{10,11... | collective-permute-start | bytes 3145736 | tf_op jit(solution)/shard_map/ppermute | solution.py:147
  223.9 4.9 %copy-start.18 = (bf16[1,1024,512]{2,1,0:T(8,128)(2,1)S(1)}, bf16[1,1024,512]{2,1,0:T(8,128)(2,1)}, u32[]{:S(2)}) copy-start(bf16[1,1024,512]{2,1,0:T(8,128)(2,1)} %copy.57) | copy-start | bytes 3145732
  223.9 6.0 %copy-start.17 = (bf16[1,1024,512]{2,1,0:T(8,128)(2,1)S(1)}, bf16[1,1024,512]{2,1,0:T(8,128)(2,1)}, u32[]{:S(2)}) copy-start(bf16[1,1024,512]{2,1,0:T(8,128)(2,1)} %copy.58) | copy-start | bytes 3145732
  223.9 7.0 %copy-start.1 = (bf16[1024,512]{1,0:T(8,128)(2,1)S(1)}, bf16[1024,512]{1,0:T(8,128)(2,1)}, u32[]{:S(2)}) copy-start(bf16[1024,512]{1,0:T(8,128)(2,1)} %copy-done) | copy-start | bytes 3145732
  223.9 7.0 %copy-start.25 = (bf16[2,512,1024]{2,1,0:T(8,128)(2,1)S(1)}, bf16[2,512,1024]{2,1,0:T(8,128)(2,1)}, u32[]{:S(2)}) copy-start(bf16[2,512,1024]{2,1,0:T(8,128)(2,1)} %pad_maximum_fusion.2) | copy-start | bytes 6291460
  225.8 32.7 %collective-permute-start.2 = (bf16[2,256,1024]{2,1,0:T(8,128)(2,1)S(1)}, bf16[2,256,1024]{2,1,0:T(8,128)(2,1)S(1)}, u32[]{:S(2)}, u32[]{:S(2)}) collective-permute-start(bf16[2,256,1024]{2,1,0:T(8,128)(2,1)S(1)} %dynamic-slice_convert_fusion.1), channel_id=1, source_target_pairs={{0,1},{1,0},{2,3},{3,2},{4,5},{5,4},{6,7},{7,6},{8,9},{9,8},{10,11... | collective-permute-start | bytes 3145736 | tf_op jit(solution)/shard_map/ppermute | solution.py:147
  230.9 6.0 %copy-start.7 = (bf16[2,256,1024]{2,1,0:T(8,128)(2,1)S(1)}, bf16[2,256,1024]{2,1,0:T(8,128)(2,1)}, u32[]{:S(2)}) copy-start(bf16[2,256,1024]{2,1,0:T(8,128)(2,1)} %param.12) | copy-start | bytes 3145732
  230.9 6.0 %copy-start.15 = (f32[1024,1024]{1,0:T(8,128)S(1)}, f32[1024,1024]{1,0:T(8,128)}, u32[]{:S(2)}) copy-start(f32[1024,1024]{1,0:T(8,128)} %copy-done.14) | copy-start | bytes 12582916
  230.9 27.7 %copy-start.22 = (bf16[2,256,1024]{2,1,0:T(8,128)(2,1)S(1)}, bf16[2,256,1024]{2,1,0:T(8,128)(2,1)}, u32[]{:S(2)}) copy-start(bf16[2,256,1024]{2,1,0:T(8,128)(2,1)} %param.23) | copy-start | bytes 3145732
  233.2 25.4 %copy-start.12 = (f32[1024,1024]{1,0:T(8,128)S(1)}, f32[1024,1024]{1,0:T(8,128)}, u32[]{:S(2)}) copy-start(f32[1024,1024]{1,0:T(8,128)} %convolution_add_fusion) | copy-start | bytes 12582916
  262.4 4.5 collective-permute-start.4
  268.1 180.2 %reduce-scatter.5.cloned.1.call-start = ((), (), s32[]{:S(2)}) async-start(), calls=%async_computation.3 | async-start | bytes 8912896 | tf_op jit(solution)/shard_map/reduce_scatter | solution.py:234
Sparse Core Ops, SparseCore 0:
  13.2 84.1 all-gather.4
  100.1 48.8 all-gather.6
  268.2 71.7 reduce-scatter.2
  344.4 103.7 reduce-scatter.4

commit v2 on v1

--- a/solution.py
+++ b/solution.py
@@ -231,7 +231,9 @@
         axis=1,
     )
     mlp_grads, attn_pack = lax.optimization_barrier((mlp_grads, attn_pack))
-    mlp_owned = lax.psum_scatter(mlp_grads, "fsdp", scatter_dimension=0, tiled=False)
+    mlp_owned = lax.psum_scatter(
+        mlp_grads.reshape(-1, hidden), "fsdp", scatter_dimension=0, tiled=True
+    )
 
     attn_parts = attn_pack.reshape(shards, 4, own_rows, local_width).transpose(1, 0, 2, 3)
     attn_parts = attn_parts.reshape(4, model_width, local_width)
@@ -280,7 +282,9 @@
         + [pad_rows(small_grads, local_width)],
         axis=1,
     )
-    attn_owned = lax.psum_scatter(attn_grads, "fsdp", scatter_dimension=0, tiled=False)
+    attn_owned = lax.psum_scatter(
+        attn_grads.reshape(-1, local_width), "fsdp", scatter_dimension=0, tiled=True
+    )
 
     attn_part = jnp.einsum("ne,de->nd", mixed_flat, dense_full, preferred_element_type=f32)
     mlp_part = jnp.einsum("nf,df->nd", act_low, out_full, preferred_element_type=f32)

time: 464 us -> 464 us (level)
  no operation moved by 1% of the time
where the time goes in v2:
time: 464 us; the launch traced here: 457 us
  waiting for transfers between devices  262 us (56%)
  matrix products  67.4 us (15%)
  local copies, waits for them, and re-layouts  46.1 us (10%)
  other arithmetic  35.4 us (8%)
  Pallas kernels  25.1 us (5%)
  between operations  14.7 us (3%)
  starting transfers between devices  7.05 us (2%)
    reduce_scatter x1, waiting for transfers between devices, on_device(): lax.psum_scatter(mlp_grads.reshape(-1, hidden), 'fsdp', scatter_dimension...  103 us
    reduce_scatter x1, waiting for transfers between devices, on_device(): lax.psum_scatter(attn_grads.reshape(-1, local_width), 'fsdp', scatter_dim...  71.3 us
    ppermute x2, waiting for transfers between devices, join_rows(): other = lax.ppermute(local, 'tp', [(0, 1), (1, 0)])  33.3 us
    all_gather x1, waiting for transfers between devices, on_device(): lax.all_gather(jnp.concatenate([mlp_in_weight, mlp_out_weight, small_rows...  30.4 us
    pallas_call x1, Pallas kernels, attention(): pl.pallas_call(attention_kernel, grid=(seq_count, pairs), in_specs=[pl.Bl...  25.1 us
    ppermute x2, waiting for transfers between devices, share_rows(): arrived = lax.ppermute(away, 'tp', [(0, 1), (1, 0)])  23.3 us
    unnamed x71, local copies, waits for them, and re-layouts  11.1 us
    dot_general x1, matrix products, on_device(): jnp.einsum('nf,df->nd', act_low, out_full, preferred_element_type=f32)  9.96 us
  transfers between devices with their start and end apart: 9, of which 7 were waited for; matrix products, arithmetic and copies ran while one was open for 23% of the time, Pallas kernels for 0%

profile of v2, /device:TPU:0, one launch (start us, length us, event | category | flops | bytes accessed | tf_op | source)
XLA Modules:
  0.0 457.3 jit_solution(9205661147843867804)
XLA Ops:
  11.1 1.9 pad_maximum_fusion.3
  13.1 3.0 collective-permute-start.1
  16.9 1.7 copy.52.seg_col
  18.7 1.4 convert_reduce_fusion.3
  20.1 1.9 multiply_sine_fusion
  22.1 1.7 concatenate.42.behind
  23.8 1.7 concatenate.41.ahead
  25.6 1.7 concatenate.40.keep
  28.7 11.7 %collective-permute-done.1 = bf16[2,256,1024]{2,1,0:T(8,128)(2,1)} collective-permute-done((bf16[2,256,1024]{2,1,0:T(8,128)(2,1)}, bf16[2,256,1024]{2,1,0:T(8,128)(2,1)}, u32[]{:S(2)}, u32[]{:S(2)}) %collective-permute-start.1) | collective-permute-done | bytes 1048608 | tf_op jit(solution)/shard_map/ppermute | solution.py:132
  40.4 21.6 %collective-permute-done = bf16[2,256,1024]{2,1,0:T(8,128)(2,1)} collective-permute-done((bf16[2,256,1024]{2,1,0:T(8,128)(2,1)}, bf16[2,256,1024]{2,1,0:T(8,128)(2,1)}, u32[]{:S(2)}, u32[]{:S(2)}) %collective-permute-start) | collective-permute-done | bytes 1048608 | tf_op jit(solution)/shard_map/ppermute | solution.py:132
  62.1 2.3 broadcast_select_fusion.1
  65.5 1.5 pad_maximum_fusion.2
  66.9 30.4 %all-gather.5.cloned.1.call-done = bf16[2304,2048]{1,0:T(8,128)(2,1)} async-done(((bf16[144,2048]{1,0:T(8,128)(2,1)}), bf16[2304,2048]{1,0:T(8,128)(2,1)}) %all-gather.5.cloned.1.call-update) | async-done | bytes 9437200 | tf_op jit(solution)/shard_map/all_gather | solution.py:187
  97.6 1.5 slice_convert_fusion
  100.3 1.3 copy-done.23
  105.0 2.3 add_convert_fusion.1
  107.3 1.2 copy-done.13
  109.8 7.4 %multiply_convert_fusion = (bf16[1024,2048]{1,0:T(8,128)(2,1)S(1)}, f32[1024,2048]{1,0:T(8,128)}) fusion(f32[2048]{0:T(1024)S(1)} %slice_bitcast_fusion.3, bf16[1024,1024]{1,0:T(8,128)(2,1)S(1)} %bitcast.143, bf16[1024,2048]{1,0:T(8,128)(2,1)S(1)} %bitcast.127), kind=kOutput, calls=%fused_computation.7 | convolution fusion | flops 4307550208 | bytes 18882560 | tf_op jit(solution)/shard_map/dot_general | solution.py:216
  117.2 6.3 %convolution_convert_fusion = bf16[1024,2048]{1,0:T(8,128)(2,1)} fusion(bf16[1024,1024]{1,0:T(8,128)(2,1)S(1)} %bitcast.138, bf16[1024,2048]{1,0:T(8,128)(2,1)S(1)} %get-tuple-element.69), kind=kOutput, calls=%fused_computation.24 | convolution fusion | flops 4297064448 | bytes 10485760 | tf_op jit(solution)/shard_map/nd,nf->df/dot_general | solution.py:225
  123.5 9.3 %fusion.34 = (bf16[2048]{0:T(1024)(128)(2,1)S(1)}, bf16[1024,2048]{1,0:T(8,128)(2,1)S(1)}) fusion(f32[1024,2048]{1,0:T(8,128)} %get-tuple-element.70, f32[2048]{0:T(1024)S(1)} %slice_bitcast_fusion.3, bf16[1024,1024]{1,0:T(8,128)(2,1)S(1)} %bitcast.139, bf16[1024,2048]{1,0:T(8,128)(2,1)S(1)} %bitcast.129), kind=kOutput, calls=%fused_computation.110 | convolution fusion | flops 4324325376 | bytes 18886656 | tf_op jit(solution)/shard_map/dot_general | solution.py:222
  132.8 6.6 %convolution_convert_fusion.1 = bf16[1024,2048]{1,0:T(8,128)(2,1)} fusion(bf16[1024,1024]{1,0:T(8,128)(2,1)S(1)} %add_convert_fusion.3, bf16[1024,2048]{1,0:T(8,128)(2,1)S(1)} %get-tuple-element.72), kind=kOutput, calls=%fused_computation.25 | convolution fusion | flops 4297064448 | bytes 10485760 | tf_op jit(solution)/shard_map/nd,nf->df/dot_general | solution.py:224
  139.4 8.4 %pad_maximum_fusion = bf16[16,128,2048]{2,1,0:T(8,128)(2,1)} fusion(bf16[16,64,2048]{2,1,0:T(8,128)(2,1)} %bitcast.131, bf16[16,64,2048]{2,1,0:T(8,128)(2,1)} %bitcast.132), kind=kLoop, calls=%fused_computation.6 | loop fusion | flops 16777216 | bytes 16777216 | tf_op jit(solution)/shard_map/concatenate | solution.py:226
  147.8 10.0 %fusion.35 = f32[1024,1024]{1,0:T(8,128)} fusion(bf16[1024,2048]{1,0:T(8,128)(2,1)} %copy-done.30, bf16[1024,2048]{1,0:T(8,128)(2,1)} %bitcast.130), kind=kOutput, calls=%fused_computation.111 | convolution fusion | flops 4294967296 | bytes 12582912 | tf_op jit(solution)/shard_map/nf,df->nd/dot_general | solution.py:290
  157.8 1.3 slice.187
  159.1 2.2 slice.185
  163.1 3.4 add_bitcast_fusion.proj
  166.6 25.1 %shard_map.203 = (bf16[1024,512]{1,0:T(8,128)(2,1)S(1)}, bf16[3,1024,512]{2,1,0:T(8,128)(2,1)S(1)}) custom-call(s32[2,1,512]{2,1,0:T(1,128)S(1)} %broadcast_in_dim.12.seg_row, s32[2,512,1]{2,1,0:T(8,128)S(1)} %copy-done.5, f32[2,512,128]{2,1,0:T(8,128)S(1)} %copy-done.4, f32[2,512,128]{2,1,0:T(8,128)S(1)} %copy-done.3, f32[2,512,128]{2,1,0:T(8,128)S(1)} %copy-done.2, ...), custom_call_target="tpu_custom_call" | custom-call | flops 6442450944 | bytes 12582912 | tf_op jit(solution)/shard_map/pallas_call | solution.py:105
  191.7 5.0 %fusion.36 = f32[1024,1024,1]{1,0,2:T(8,128)} fusion(bf16[3,1024,512]{2,1,0:T(8,128)(2,1)S(1)} %get-tuple-element.21, bf16[3,1024,512]{2,1,0:T(8,128)(2,1)S(1)} %bitcast.134), kind=kOutput, calls=%fused_computation.112 | convolution fusion | flops 3221225472 | bytes 10485760 | tf_op jit(solution)/shard_map/jne,jde->nd/dot_general | solution.py:250
  196.7 9.0 %fusion.30 = (f32[1024]{0:T(1024)S(1)}, f32[1024]{0:T(1024)S(1)}, f32[1024,1024]{1,0:T(8,128)S(1)}, f32[1024]{0:T(1024)S(1)}, f32[1024]{0:T(1024)S(1)}, /*index=5*/bf16[1024,1024]{1,0:T(8,128)(2,1)S(1)}) fusion(f32[1024]{0:T(1024)S(1)} %bitcast.159, f32[1024]{0:T(1024)S(1)} %bitcast.157, bf16[2,256,1024]{2,1,0:T(8,128)(2,1)S(1)} %copy-done.9, ...), kind=kOutput, calls=%fused_computation.106 | convolution fusion | flops 4313837568 | bytes 21008384 | tf_op jit(solution)/shard_map/nf,df->nd/dot_general | solution.py:251
  205.7 3.7 convert_bitcast_fusion
  210.6 1.5 collective-permute-start.3
  212.1 3.2 convolution_add_fusion
  215.3 1.8 fusion.32
  217.1 2.3 copy.56
  219.4 2.3 copy.55
  221.6 2.3 copy.54
  223.9 1.9 dynamic-slice_convert_fusion.1
  226.5 2.3 constant_dynamic-update-slice_fusion.4
  230.9 2.3 convolution_convert_fusion.2
  233.2 3.7 collective-permute-done.3
  236.9 2.0 fusion.20
  239.0 19.6 %collective-permute-done.2 = bf16[2,256,1024]{2,1,0:T(8,128)(2,1)S(1)} collective-permute-done((bf16[2,256,1024]{2,1,0:T(8,128)(2,1)S(1)}, bf16[2,256,1024]{2,1,0:T(8,128)(2,1)S(1)}, u32[]{:S(2)}, u32[]{:S(2)}) %collective-permute-start.2) | collective-permute-done | bytes 1048608 | tf_op jit(solution)/shard_map/ppermute | solution.py:147
  258.6 3.8 convert_reduce_fusion.2
  262.4 1.5 collective-permute-start.4
  263.9 2.3 constant_dynamic-update-slice_fusion.1
  268.7 71.3 %reduce-scatter.3.cloned.1.call-done = bf16[272,512]{1,0:T(8,128)(2,1)} async-done(((bf16[4352,512]{1,0:T(8,128)(2,1)}), bf16[272,512]{1,0:T(8,128)(2,1)}) %reduce-scatter.3.cloned.1.call-update) | async-done | bytes 278544 | tf_op jit(solution)/shard_map/reduce_scatter | solution.py:285
  345.6 102.6 %reduce-scatter.5.cloned.1.call-done = bf16[128,2048]{1,0:T(8,128)(2,1)} async-done(((bf16[2048,2048]{1,0:T(8,128)(2,1)}), bf16[128,2048]{1,0:T(8,128)(2,1)}) %reduce-scatter.5.cloned.1.call-update) | async-done | bytes 524304 | tf_op jit(solution)/shard_map/reduce_scatter | solution.py:234
  448.3 2.1 slice_convert_fusion.1
  (147 shorter events, 27.3 us)
Async XLA Ops:
  7.2 90.2 %all-gather.5.cloned.1.call-start = ((), (), s32[]{:S(2)}) async-start(), calls=%async_computation.4 | async-start | bytes 10027008 | tf_op jit(solution)/shard_map/all_gather | solution.py:187
  13.0 144.7 %all-gather.7.cloned.1.call-start = ((), (), s32[]{:S(2)}) async-start(), calls=%async_computation.5 | async-start | bytes 4456448 | tf_op jit(solution)/shard_map/all_gather | solution.py:196
  13.1 27.3 %collective-permute-start.1 = (bf16[2,256,1024]{2,1,0:T(8,128)(2,1)}, bf16[2,256,1024]{2,1,0:T(8,128)(2,1)}, u32[]{:S(2)}, u32[]{:S(2)}) collective-permute-start(bf16[2,256,1024]{2,1,0:T(8,128)(2,1)} %param.23), channel_id=1, source_target_pairs={{0,1},{1,0},{2,3},{3,2},{4,5},{5,4},{6,7},{7,6},{8,9},{9,8},{10,11... | collective-permute-start | bytes 3145736 | tf_op jit(solution)/shard_map/ppermute | solution.py:132
  16.1 45.9 %collective-permute-start = (bf16[2,256,1024]{2,1,0:T(8,128)(2,1)}, bf16[2,256,1024]{2,1,0:T(8,128)(2,1)}, u32[]{:S(2)}, u32[]{:S(2)}) collective-permute-start(bf16[2,256,1024]{2,1,0:T(8,128)(2,1)} %param.12), channel_id=1, source_target_pairs={{0,1},{1,0},{2,3},{3,2},{4,5},{5,4},{6,7},{7,6},{8,9},{9,8},{10,11... | collective-permute-start | bytes 3145736 | tf_op jit(solution)/shard_map/ppermute | solution.py:132
  23.8 3.5 copy-start.27
  23.8 3.6 copy-start.28
  23.8 4.3 copy-start.6
  64.3 40.7 %copy-start.8 = (bf16[2,256,1024]{2,1,0:T(8,128)(2,1)}, bf16[2,256,1024]{2,1,0:T(8,128)(2,1)S(1)}, u32[]{:S(2)}) copy-start(bf16[2,256,1024]{2,1,0:T(8,128)(2,1)S(1)} %get-tuple-element.73) | copy-start | bytes 3145732
  64.4 40.7 %copy-start.10 = (bf16[2,256,1024]{2,1,0:T(8,128)(2,1)}, bf16[2,256,1024]{2,1,0:T(8,128)(2,1)S(1)}, u32[]{:S(2)}) copy-start(bf16[2,256,1024]{2,1,0:T(8,128)(2,1)S(1)} %get-tuple-element.74) | copy-start | bytes 3145732
  97.4 242.6 %reduce-scatter.3.cloned.1.call-start = ((), (), s32[]{:S(2)}) async-start(), calls=%async_computation.2 | async-start | bytes 4734976 | tf_op jit(solution)/shard_map/reduce_scatter | solution.py:285
  100.3 1.3 copy-start.23
  103.9 4.6 %copy-start.13 = (bf16[2304,2048]{1,0:T(8,128)(2,1)S(1)}, bf16[2304,2048]{1,0:T(8,128)(2,1)}, u32[]{:S(2)}) copy-start(bf16[2304,2048]{1,0:T(8,128)(2,1)} %all-gather.5.cloned.1.call-done) | copy-start | bytes 28311556
  109.7 7.4 %copy-start.19 = (bf16[16,64,2048]{2,1,0:T(8,128)(2,1)}, bf16[16,64,2048]{2,1,0:T(8,128)(2,1)S(1)}, u32[]{:S(2)}) copy-start(bf16[16,64,2048]{2,1,0:T(8,128)(2,1)S(1)} %get-tuple-element.36) | copy-start | bytes 12582916
  109.8 13.7 %copy-start.21 = (bf16[16,64,2048]{2,1,0:T(8,128)(2,1)}, bf16[16,64,2048]{2,1,0:T(8,128)(2,1)S(1)}, u32[]{:S(2)}) copy-start(bf16[16,64,2048]{2,1,0:T(8,128)(2,1)S(1)} %get-tuple-element.35) | copy-start | bytes 12582916
  109.8 7.4 %copy-start.24 = (bf16[2,512,1024]{2,1,0:T(8,128)(2,1)S(1)}, bf16[2,512,1024]{2,1,0:T(8,128)(2,1)}, u32[]{:S(2)}) copy-start(bf16[2,512,1024]{2,1,0:T(8,128)(2,1)} %pad_maximum_fusion.2) | copy-start | bytes 6291460
  117.2 6.3 %copy-start.30 = (bf16[1024,2048]{1,0:T(8,128)(2,1)}, bf16[1024,2048]{1,0:T(8,128)(2,1)S(1)}, u32[]{:S(2)}) copy-start(bf16[1024,2048]{1,0:T(8,128)(2,1)S(1)} %get-tuple-element.69) | copy-start | bytes 12582916
  132.8 6.6 %copy-start.29 = (bf16[1024,2048]{1,0:T(8,128)(2,1)}, bf16[1024,2048]{1,0:T(8,128)(2,1)S(1)}, u32[]{:S(2)}) copy-start(bf16[1024,2048]{1,0:T(8,128)(2,1)S(1)} %get-tuple-element.72) | copy-start | bytes 12582916
  161.5 1.6 copy-start.26
  163.1 3.4 copy-start.2
  163.1 3.4 copy-start.3
  163.1 3.5 copy-start.4
  163.1 3.5 copy-start.5
  191.7 20.4 %copy-start = (bf16[1024,512]{1,0:T(8,128)(2,1)}, bf16[1024,512]{1,0:T(8,128)(2,1)S(1)}, u32[]{:S(2)}) copy-start(bf16[1024,512]{1,0:T(8,128)(2,1)S(1)} %get-tuple-element.20) | copy-start | bytes 3145732
  191.7 5.1 %copy-start.9 = (bf16[2,256,1024]{2,1,0:T(8,128)(2,1)S(1)}, bf16[2,256,1024]{2,1,0:T(8,128)(2,1)}, u32[]{:S(2)}) copy-start(bf16[2,256,1024]{2,1,0:T(8,128)(2,1)} %copy-done.8) | copy-start | bytes 3145732
  191.7 5.0 %copy-start.11 = (bf16[2,256,1024]{2,1,0:T(8,128)(2,1)S(1)}, bf16[2,256,1024]{2,1,0:T(8,128)(2,1)}, u32[]{:S(2)}) copy-start(bf16[2,256,1024]{2,1,0:T(8,128)(2,1)} %copy-done.10) | copy-start | bytes 3145732
  191.7 5.0 %copy-start.20 = (bf16[16,64,2048]{2,1,0:T(8,128)(2,1)S(1)}, bf16[16,64,2048]{2,1,0:T(8,128)(2,1)}, u32[]{:S(2)}) copy-start(bf16[16,64,2048]{2,1,0:T(8,128)(2,1)} %copy-done.19) | copy-start | bytes 12582916
  205.7 3.8 copy-start.14
  205.7 6.4 %copy-start.16 = (f32[1024,1024]{1,0:T(8,128)S(1)}, f32[1024,1024]{1,0:T(8,128)}, u32[]{:S(2)}) copy-start(f32[1024,1024]{1,0:T(8,128)} %fusion.35) | copy-start | bytes 12582916
  210.6 26.3 %collective-permute-start.3 = (bf16[2,256,1024]{2,1,0:T(8,128)(2,1)}, bf16[2,256,1024]{2,1,0:T(8,128)(2,1)}, u32[]{:S(2)}, u32[]{:S(2)}) collective-permute-start(bf16[2,256,1024]{2,1,0:T(8,128)(2,1)} %dynamic-slice_convert_fusion), channel_id=1, source_target_pairs={{0,1},{1,0},{2,3},{3,2},{4,5},{5,4},{6,7},{7,6},{8,9},{9,8},{10,11... | collective-permute-start | bytes 3145736 | tf_op jit(solution)/shard_map/ppermute | solution.py:147
  223.9 4.9 %copy-start.18 = (bf16[1,1024,512]{2,1,0:T(8,128)(2,1)S(1)}, bf16[1,1024,512]{2,1,0:T(8,128)(2,1)}, u32[]{:S(2)}) copy-start(bf16[1,1024,512]{2,1,0:T(8,128)(2,1)} %copy.55) | copy-start | bytes 3145732
  223.9 6.0 %copy-start.17 = (bf16[1,1024,512]{2,1,0:T(8,128)(2,1)S(1)}, bf16[1,1024,512]{2,1,0:T(8,128)(2,1)}, u32[]{:S(2)}) copy-start(bf16[1,1024,512]{2,1,0:T(8,128)(2,1)} %copy.56) | copy-start | bytes 3145732
  223.9 7.0 %copy-start.1 = (bf16[1024,512]{1,0:T(8,128)(2,1)S(1)}, bf16[1024,512]{1,0:T(8,128)(2,1)}, u32[]{:S(2)}) copy-start(bf16[1024,512]{1,0:T(8,128)(2,1)} %copy-done) | copy-start | bytes 3145732
  223.9 7.0 %copy-start.25 = (bf16[2,512,1024]{2,1,0:T(8,128)(2,1)S(1)}, bf16[2,512,1024]{2,1,0:T(8,128)(2,1)}, u32[]{:S(2)}) copy-start(bf16[2,512,1024]{2,1,0:T(8,128)(2,1)} %pad_maximum_fusion.2) | copy-start | bytes 6291460
  225.8 32.7 %collective-permute-start.2 = (bf16[2,256,1024]{2,1,0:T(8,128)(2,1)S(1)}, bf16[2,256,1024]{2,1,0:T(8,128)(2,1)S(1)}, u32[]{:S(2)}, u32[]{:S(2)}) collective-permute-start(bf16[2,256,1024]{2,1,0:T(8,128)(2,1)S(1)} %dynamic-slice_convert_fusion.1), channel_id=1, source_target_pairs={{0,1},{1,0},{2,3},{3,2},{4,5},{5,4},{6,7},{7,6},{8,9},{9,8},{10,11... | collective-permute-start | bytes 3145736 | tf_op jit(solution)/shard_map/ppermute | solution.py:147
  230.9 6.0 %copy-start.7 = (bf16[2,256,1024]{2,1,0:T(8,128)(2,1)S(1)}, bf16[2,256,1024]{2,1,0:T(8,128)(2,1)}, u32[]{:S(2)}) copy-start(bf16[2,256,1024]{2,1,0:T(8,128)(2,1)} %param.12) | copy-start | bytes 3145732
  230.9 6.0 %copy-start.15 = (f32[1024,1024]{1,0:T(8,128)S(1)}, f32[1024,1024]{1,0:T(8,128)}, u32[]{:S(2)}) copy-start(f32[1024,1024]{1,0:T(8,128)} %copy-done.14) | copy-start | bytes 12582916
  230.9 27.7 %copy-start.22 = (bf16[2,256,1024]{2,1,0:T(8,128)(2,1)S(1)}, bf16[2,256,1024]{2,1,0:T(8,128)(2,1)}, u32[]{:S(2)}) copy-start(bf16[2,256,1024]{2,1,0:T(8,128)(2,1)} %param.23) | copy-start | bytes 3145732
  233.2 25.4 %copy-start.12 = (f32[1024,1024]{1,0:T(8,128)S(1)}, f32[1024,1024]{1,0:T(8,128)}, u32[]{:S(2)}) copy-start(f32[1024,1024]{1,0:T(8,128)} %convolution_add_fusion) | copy-start | bytes 12582916
  262.4 4.5 collective-permute-start.4
  268.1 180.2 %reduce-scatter.5.cloned.1.call-start = ((), (), s32[]{:S(2)}) async-start(), calls=%async_computation.3 | async-start | bytes 8912896 | tf_op jit(solution)/shard_map/reduce_scatter | solution.py:234
Sparse Core Ops, SparseCore 0:
  13.2 84.1 all-gather.4
  100.1 48.8 all-gather.6
  268.2 71.7 reduce-scatter.2
  344.4 103.7 reduce-scatter.4
